TPU v7x, 128 devices: a whole 4x4x4 slice. The times are simulated.
128 devices in a mesh: group: 8 (over x_lo, y), tensor: 16 (over x_hi, z, core).
Axes of the slice: x: 4 (x_hi: 2, x_lo: 2; x = x_hi * 2 + x_lo), y: 4, z: 4, core: 2. Of those that a mesh axis runs over, the one named last changes fastest.
Arguments:
- backbone_hidden: bfloat16 [1024, 27648], P('group', 'tensor'), may hold values from -6 to 6
- backbone_down: bfloat16 [27648, 5120], P('tensor', 'group'), may hold values from -0.0390625 to 0.0390625
- residual: bfloat16 [1024, 5120], P(None, 'group'), may hold values from -6 to 6
- head_grad: bfloat16 [1024, 5120], P(None, 'group'), may hold values from -6 to 6
- gain: float32 [4, 5120], replicated, may hold values from 0.1 to 1.9
- w_up: bfloat16 [5120, 55296], P(None, ('group', 'tensor')), may hold values from -0.078125 to 0.078125
- w_down: bfloat16 [55296, 5120], P(('group', 'tensor')), may hold values from -0.0546875 to 0.0546875
- route: int32 [16, 4, 24], replicated, may hold values from -1 to 63, as said below
Outputs:
- grad_hidden: bfloat16 [1024, 27648], P('group', 'tensor')
- grad_backbone: bfloat16 [27648, 5120], P('tensor', 'group')
- grad_up: bfloat16 [5120, 55296], P(None, ('group', 'tensor'))
- grad_down: bfloat16 [55296, 5120], P(('group', 'tensor'))
Inputs may be any that keep to these rules, and one draw needn't show every extreme that they name: route[b, h, :] holds first the positions, within the b-th aligned block of 64 tokens, of the tokens of dataset h in that block (each position once), then -1 in the remaining slots; every token of a block belongs to exactly one dataset; in every block some dataset has exactly 24 tokens.
All inputs are finite; a program needn't handle non-finite values.
Results may differ from a plain program's by a relative error of at most 0.024.
Values may be sent and summed in bfloat16 or wider, within the bound.
A program may use at most 128 MiB of HBM per device.

v0:
```python
import jax
import jax.numpy as jnp
from jax import lax
from jax.sharding import PartitionSpec as P


def norm_backward(d_normed, rows_f, inv_rms, scale_row, model_width):
    scaled = d_normed * scale_row
    inner = jnp.sum(rows_f * scaled, axis=-1, keepdims=True)
    return inv_rms * scaled - rows_f * inv_rms**3 * (inner / model_width)


def local(backbone_hidden, backbone_down, residual, head_grad, gain, w_up, w_down, route):
    groups = lax.axis_size("group")
    head_count = gain.shape[0]
    model_width = gain.shape[1]
    pair_size = groups // head_count
    dataset = lax.axis_index("group") // pair_size
    blocks = route.shape[0]
    slot_count = route.shape[2]
    tokens = residual.shape[0]
    block_len = tokens // blocks
    slice_width = residual.shape[1]
    hidden_all = lax.all_gather(backbone_hidden, "group", axis=0, tiled=True)
    partial_value = jnp.dot(hidden_all, backbone_down, preferred_element_type=jnp.float32)
    summed = lax.psum(partial_value, "tensor")
    stream = (residual.astype(jnp.float32) + summed).astype(jnp.bfloat16)
    places = lax.broadcasted_iota(jnp.int32, (blocks, head_count, slot_count, block_len), 3)
    dataset_selector = route[:, :, :, None] == places
    select_low = dataset_selector.astype(jnp.bfloat16)
    picked_rows = jnp.einsum(
        "yija,yac->iyjc",
        select_low,
        stream.reshape(blocks, block_len, slice_width),
        preferred_element_type=jnp.float32,
    ).astype(jnp.bfloat16)
    picked_cots = jnp.einsum(
        "yija,yac->iyjc",
        select_low,
        head_grad.reshape(blocks, block_len, slice_width),
        preferred_element_type=jnp.float32,
    ).astype(jnp.bfloat16)

    def outgoing(picked):
        per_head = picked.reshape(head_count, blocks * slot_count, slice_width)
        return jnp.repeat(per_head, pair_size, axis=0).reshape(
            groups * blocks * slot_count, slice_width
        )

    head_rows, cot_rows = (
        lax.all_to_all(outgoing(picked_rows), "group", split_axis=0, concat_axis=1, tiled=True),
        lax.all_to_all(outgoing(picked_cots), "group", split_axis=0, concat_axis=1, tiled=True),
    )
    rows_f = head_rows.astype(jnp.float32)
    inv_rms = lax.rsqrt(jnp.mean(rows_f * rows_f, axis=-1, keepdims=True) + 1e-06)
    scale_row = lax.dynamic_index_in_dim(gain, dataset, 0, keepdims=False)
    normed = (rows_f * inv_rms * scale_row).astype(jnp.bfloat16)
    pre_act = jnp.dot(normed, w_up, preferred_element_type=jnp.float32)
    sigmoid = jax.nn.sigmoid(pre_act)
    hidden_act = (pre_act * sigmoid).astype(jnp.bfloat16)
    d_act = lax.dot_general(
        cot_rows, w_down, (((1,), (1,)), ((), ())), preferred_element_type=jnp.float32
    )
    d_pre = (d_act * sigmoid * (1.0 + pre_act * (1.0 - sigmoid))).astype(jnp.bfloat16)
    grad_down = lax.dot_general(
        hidden_act, cot_rows, (((0,), (0,)), ((), ())), preferred_element_type=jnp.float32
    ).astype(jnp.bfloat16)
    grad_up = lax.dot_general(
        normed, d_pre, (((0,), (0,)), ((), ())), preferred_element_type=jnp.float32
    ).astype(jnp.bfloat16)
    d_normed = lax.dot_general(
        d_pre, w_up, (((1,), (1,)), ((), ())), preferred_element_type=jnp.float32
    )
    d_summed = lax.psum(d_normed.astype(jnp.bfloat16), "tensor").astype(jnp.float32)
    d_rows = norm_backward(d_summed, rows_f, inv_rms, scale_row, model_width)
    returned_rows = lax.all_to_all(
        d_rows.astype(jnp.bfloat16), "group", split_axis=1, concat_axis=0, tiled=True
    ).astype(d_rows.dtype)
    returned_rows = returned_rows.reshape(
        head_count, pair_size, blocks, slot_count, slice_width
    ).sum(axis=1)
    scattered = jnp.einsum(
        "lret,rlez->ltz",
        dataset_selector.astype(jnp.float32),
        returned_rows,
        precision=lax.Precision.HIGHEST,
    )
    residual_gradient = (
        head_grad.astype(jnp.float32) + scattered.reshape(tokens, slice_width)
    ).astype(jnp.bfloat16)
    grad_backbone = lax.dot_general(
        hidden_all, residual_gradient, (((0,), (0,)), ((), ())), preferred_element_type=jnp.float32
    ).astype(jnp.bfloat16)
    grad_hidden = lax.psum_scatter(
        lax.dot_general(
            residual_gradient,
            backbone_down,
            (((1,), (1,)), ((), ())),
            preferred_element_type=jnp.float32,
        ).astype(jnp.bfloat16),
        "group",
        scatter_dimension=0,
        tiled=True,
    )
    return (grad_hidden, grad_backbone, grad_up, grad_down)


def solution(mesh):
    placed = (
        P("group", "tensor"),
        P("tensor", "group"),
        P(None, "group"),
        P(None, "group"),
        P(),
        P(None, ("group", "tensor")),
        P(("group", "tensor"), None),
        P(),
    )
    return jax.shard_map(
        local,
        mesh=mesh,
        in_specs=placed,
        out_specs=(
            P("group", "tensor"),
            P("tensor", "group"),
            P(None, ("group", "tensor")),
            P(("group", "tensor"), None),
        ),
        check_vma=False,
    )
```

profile of v0, /device:TPU:1, one launch (start us, length us, event | category | flops | bytes accessed | tf_op | source)
XLA Modules:
  0.0 627.1 jit_solution(11336978759483696821)
XLA Ops:
  7.2 0.0 copy-start
  7.2 0.0 all-gather.2.cloned.1.call-start
  7.2 0.7 all-gather.2.cloned.1.call-update
  7.9 0.0 all-reduce.3.cloned.1.call-start
  8.0 56.0 %all-gather.2.cloned.1.call-done = bf16[1024,1728]{0,1:T(8,128)(2,1)} async-done(((bf16[128,1728]{0,1:T(8,128)(2,1)}), bf16[1024,1728]{0,1:T(8,128)(2,1)}) %all-gather.2.cloned.1.call-update) | async-done | bytes 3538960 | tf_op jit(solution)/shard_map/all_gather | solution.py:24
  64.0 6.6 %fusion.13 = f32[1024,640]{1,0:T(8,128)} fusion(bf16[1024,1728]{0,1:T(8,128)(2,1)} %all-gather.2.cloned.1.call-done, bf16[1728,640]{1,0:T(8,128)(2,1)S(1)} %copy-done), kind=kOutput, calls=%fused_computation.37 | convolution fusion | flops 2264924160 | bytes 8372224 | tf_op jit(solution)/shard_map/dot_general | solution.py:25
  70.6 0.0 all-reduce.3.cloned.1.call-update
  70.6 150.4 %all-reduce.3.cloned.1.call-done = f32[1024,640]{1,0:T(8,128)} async-done(((f32[1024,640]{1,0:T(8,128)}), f32[1024,640]{1,0:T(8,128)}) %all-reduce.3.cloned.1.call-update) | async-done | bytes 2621456 | tf_op jit(solution)/shard_map/psum | solution.py:26
  221.0 2.0 add_convert_fusion
  223.0 0.7 convert_bitcast_fusion.2
  223.8 0.2 copy.16
  223.9 2.3 broadcast_in_dim.4
  226.2 4.7 all-to-all-start
  230.9 0.7 convert_bitcast_fusion.1
  231.7 1.4 copy.17
  233.1 4.0 copy.18
  237.1 39.6 %all-to-all-done = bf16[8,384,640]{2,1,0:T(8,128)(2,1)} async-done(((bf16[8,384,640]{2,1,0:T(8,128)(2,1)}), bf16[8,384,640]{2,1,0:T(8,128)(2,1)}, u32[]{:S(2)}, u32[]{:S(2)}) %all-to-all-start) | async-done | bytes 3932192 | tf_op jit(solution)/shard_map/all_to_all | solution.py:51
  276.7 3.8 broadcast_in_dim.5
  280.5 4.6 all-to-all-start.1
  285.1 0.2 all-reduce.5.cloned.1.call-start
  285.3 0.9 constant_dynamic-slice_fusion
  286.3 2.8 convert_bitcast_fusion
  289.1 1.0 copy.31
  290.1 5.8 fusion
  295.9 2.5 fusion.12
  298.5 32.4 %all-to-all-done.1 = bf16[8,384,640]{1,2,0:T(8,128)(2,1)} async-done(((bf16[8,384,640]{1,2,0:T(8,128)(2,1)}), bf16[8,384,640]{1,2,0:T(8,128)(2,1)}, u32[]{:S(2)}, u32[]{:S(2)}) %all-to-all-start.1) | async-done | bytes 3932192 | tf_op jit(solution)/shard_map/all_to_all | solution.py:52
  330.9 6.1 fusion.6
  337.0 4.2 convolution_convert_fusion.2
  341.2 0.0 all-reduce.5.cloned.1.call-update
  341.2 0.0 reduce-scatter.4.cloned.1.call-start
  341.3 146.6 %all-reduce.5.cloned.1.call-done = bf16[384,5120]{1,0:T(8,128)(2,1)} async-done(((bf16[384,5120]{1,0:T(8,128)(2,1)}), bf16[384,5120]{1,0:T(8,128)(2,1)}) %all-reduce.5.cloned.1.call-update) | async-done | bytes 3932176 | tf_op jit(solution)/shard_map/psum | solution.py:74
  487.9 5.7 multiply_reduce_fusion
  493.6 5.0 subtract_convert_fusion
  498.6 0.4 copy.35
  498.9 48.1 %all_to_all.45 = bf16[384,8,640]{2,0,1:T(8,128)(2,1)S(1)} all-to-all(bf16[384,8,640]{2,0,1:T(8,128)(2,1)S(1)} %bitcast.70), channel_id=1, replica_groups=mesh['group'=8,'tensor'=16] {'group'}, dimensions={1} | all-to-all | bytes 7864320 | tf_op jit(solution)/shard_map/all_to_all | solution.py:76
  547.1 3.7 convert_element_type.111
  550.7 6.1 reduce_sum.29
  556.8 4.3 fusion.1
  561.1 0.3 fusion.4
  561.4 1.0 copy-done.6
  562.5 4.4 convolution_convert_fusion.3
  566.8 5.8 copy.26
  572.7 0.0 reduce-scatter.4.cloned.1.call-update
  572.7 6.7 %convolution_convert_fusion.1 = bf16[432,5120]{1,0:T(8,128)(2,1)} fusion(bf16[384,5120]{0,1:T(8,128)(2,1)} %bitcast.13, f32[384,432]{0,1:T(8,128)S(1)} %fusion.12), kind=kOutput, calls=%fused_computation.8 | convolution fusion | flops 1701734400 | bytes 9019392 | tf_op jit(solution)/shard_map/dot_general | solution.py:65
  579.4 8.4 %convolution_convert_fusion = bf16[5120,432]{0,1:T(8,128)(2,1)} fusion(bf16[384,432]{0,1:T(8,128)(2,1)S(1)} %fusion.6, f32[384,5120]{1,0:T(8,128)} %bitcast.61, f32[5120]{0:T(1024)S(1)} %bitcast.78, f32[384]{0:T(512)S(1)} %get-tuple-element.5), kind=kOutput, calls=%fused_computation.7 | convolution fusion | flops 1706803200 | bytes 12641792 | tf_op jit(solution)/shard_map/dot_general | solution.py:68
  587.8 4.1 fusion.3
  591.9 26.7 %reduce-scatter.4.cloned.1.call-done = bf16[128,1728]{1,0:T(8,128)(2,1)} async-done(((bf16[1024,1728]{1,0:T(8,128)(2,1)}), bf16[128,1728]{1,0:T(8,128)(2,1)}) %reduce-scatter.4.cloned.1.call-update) | async-done | bytes 442384
  618.6 2.0 copy.27
  (30 shorter events, 0.1 us)
Async XLA Ops:
  7.2 56.8 %copy-start = (bf16[1728,640]{1,0:T(8,128)(2,1)S(1)}, bf16[1728,640]{1,0:T(8,128)(2,1)}, u32[]{:S(2)}) copy-start(bf16[1728,640]{1,0:T(8,128)(2,1)} %param.9) | copy-start | bytes 6635524
  7.2 56.8 %all-gather.2.cloned.1.call-start = ((), (), s32[]{:S(2)}) async-start(), calls=%async_computation.4 | async-start | bytes 3981312 | tf_op jit(solution)/shard_map/all_gather | solution.py:24
  7.9 213.1 %copy-start.5 = (bf16[1024,640]{1,0:T(8,128)(2,1)S(1)}, bf16[1024,640]{1,0:T(8,128)(2,1)}, u32[]{:S(2)}) copy-start(bf16[1024,640]{1,0:T(8,128)(2,1)} %param.10) | copy-start | bytes 3932164
  7.9 213.1 %all-reduce.3.cloned.1.call-start = ((), (), s32[]{:S(2)}) async-start(), calls=%async_computation.5 | async-start | bytes 5242880 | tf_op jit(solution)/shard_map/psum | solution.py:26
  70.6 152.5 %copy-start.8 = (s32[16,4,24]{2,1,0:T(4,128)S(1)}, s32[16,4,24]{2,1,0:T(4,128)}, u32[]{:S(2)}) copy-start(s32[16,4,24]{2,1,0:T(4,128)} %param.15) | copy-start | bytes 18436
  226.2 4.7 copy-start.3
  226.2 50.5 %all-to-all-start = ((bf16[8,384,640]{2,1,0:T(8,128)(2,1)}), bf16[8,384,640]{2,1,0:T(8,128)(2,1)}, u32[]{:S(2)}, u32[]{:S(2)}) async-start(bf16[8,384,640]{2,1,0:T(8,128)(2,1)} %bitcast.68), calls=%async_computation | async-start | bytes 7864320 | tf_op jit(solution)/shard_map/all_to_all | solution.py:51
  280.5 50.4 %all-to-all-start.1 = ((bf16[8,384,640]{1,2,0:T(8,128)(2,1)}), bf16[8,384,640]{1,2,0:T(8,128)(2,1)}, u32[]{:S(2)}, u32[]{:S(2)}) async-start(bf16[8,384,640]{1,2,0:T(8,128)(2,1)} %bitcast.67), calls=%async_computation.1 | async-start | bytes 7864320 | tf_op jit(solution)/shard_map/all_to_all | solution.py:52
  285.1 202.8 %all-reduce.5.cloned.1.call-start = ((), (), s32[]{:S(2)}) async-start(), calls=%async_computation.6 | async-start | bytes 7864320 | tf_op jit(solution)/shard_map/psum | solution.py:74
  286.2 9.7 %slice-start = ((s8[4423680]{0:T(1024)(128)(4,1)}), s8[4194304]{0:T(1024)(128)(4,1)S(1)}, s32[]{:S(2)}) async-start(s8[4423680]{0:T(1024)(128)(4,1)} %bitcast.63), calls=%async_computation.8 | async-start | bytes 8388608
  289.0 6.9 %slice-start.1 = ((s8[4423680]{0:T(1024)(128)(4,1)}), s8[229376]{0:T(1024)(128)(4,1)S(1)}, s32[]{:S(2)}) async-start(s8[4423680]{0:T(1024)(128)(4,1)} %bitcast.63), calls=%async_computation.9 | async-start | bytes 458752
  290.1 5.8 copy-start.1
  295.9 41.1 %slice-start.2 = ((s8[4423680]{0:T(1024)(128)(4,1)}), s8[229376]{0:T(1024)(128)(4,1)S(1)}, s32[]{:S(2)}) async-start(s8[4423680]{0:T(1024)(128)(4,1)} %bitcast.65), calls=%async_computation.10 | async-start | bytes 458752
  330.9 6.1 slice-start.3
  341.2 277.3 %reduce-scatter.4.cloned.1.call-start = ((), (), s32[]{:S(2)}) async-start(), calls=%async_computation.7 | async-start | bytes 4128768
  487.9 5.7 copy-start.2
  556.8 4.3 copy-start.4
  561.4 1.1 copy-start.6
  579.4 8.4 %copy-start.7 = (bf16[1024,640]{1,0:T(8,128)(2,1)S(1)}, bf16[1024,640]{1,0:T(8,128)(2,1)}, u32[]{:S(2)}) copy-start(bf16[1024,640]{1,0:T(8,128)(2,1)} %copy-done.6) | copy-start | bytes 3932164
  579.4 8.4 %copy-start.9 = (bf16[1024,1728]{0,1:T(8,128)(2,1)S(1)}, bf16[1024,1728]{0,1:T(8,128)(2,1)}, u32[]{:S(2)}) copy-start(bf16[1024,1728]{0,1:T(8,128)(2,1)} %all-gather.2.cloned.1.call-done) | copy-start | bytes 10616836
Sparse Core Ops, SparseCore 0:
  9.6 54.3 all-gather.1
  70.7 150.2 all-reduce.2
  341.3 146.4 all-reduce.4
  572.8 45.6 reduce-scatter.3
where the time goes:
time: 629 us; the launch traced here: 627 us
  waiting for transfers between devices  453 us (72%)
  matrix products  48.6 us (8%)
  blocking collectives  48.1 us (8%)
  other arithmetic  31.3 us (5%)
  local copies, waits for them, and re-layouts  22.9 us (4%)
  between operations  14 us (2%)
  starting transfers between devices  9.6 us (2%)
    psum x1, waiting for transfers between devices, local(): summed = lax.psum(partial_value, 'tensor')  150 us
    psum x1, waiting for transfers between devices, local(): lax.psum(d_normed.astype(jnp.bfloat16), 'tensor').astype(jnp.float32)  147 us
    all_gather x1, waiting for transfers between devices, local(): hidden_all = lax.all_gather(backbone_hidden, 'group', axis=0, tiled=True)  56 us
    all_to_all x1, blocking collectives, local(): lax.all_to_all(d_rows.astype(jnp.bfloat16), 'group', split_axis=1, concat...  48.1 us
    all_to_all x1, waiting for transfers between devices, local(): lax.all_to_all(outgoing(picked_rows), 'group', split_axis=0, concat_axis=...  39.6 us
    all_to_all x1, waiting for transfers between devices, local(): lax.all_to_all(outgoing(picked_cots), 'group', split_axis=0, concat_axis=...  32.4 us
    unnamed x5, waiting for transfers between devices  27.4 us
  transfers between devices with their start and end apart: 6, of which 6 were waited for; matrix products, arithmetic and copies ran while one was open for 6% of the time, Pallas kernels for 0%

commit v1 on v0

--- a/solution.py
+++ b/solution.py
@@ -1,7 +1,306 @@
 import jax
 import jax.numpy as jnp
 from jax import lax
+from jax.experimental import pallas as pl
+from jax.experimental.pallas import tpu as pltpu
 from jax.sharding import PartitionSpec as P
+
+MESH = pl.DeviceIdType.MESH
+F32 = jnp.float32
+BF16 = jnp.bfloat16
+GROUPS = 8
+ZC = 8
+
+
+def place():
+    g = lax.axis_index("group")
+    t = lax.axis_index("tensor")
+    return g // 4, g % 4, t // 8, (t // 2) % 4, t % 2
+
+
+def gid(xl, y):
+    return xl * 4 + lax.rem(y, 4)
+
+
+def tid(xh, z, c):
+    return xh * 8 + lax.rem(z, 4) * 2 + c
+
+
+class Copies:
+    def __init__(self, send, recv):
+        self.send, self.recv, self.made = send, recv, {}
+
+    def start(self, k, src, dst, dev):
+        cp = pltpu.make_async_remote_copy(
+            src_ref=src, dst_ref=dst, send_sem=self.send.at[k], recv_sem=self.recv.at[k],
+            device_id=dev, device_id_type=MESH,
+        )
+        cp.start()
+        self.made[k] = cp
+
+    def arrived(self, *ks):
+        for k in ks:
+            self.made[k].wait_recv()
+
+    def finish(self):
+        for cp in self.made.values():
+            cp.wait_send()
+
+
+def enter(peers):
+    barrier = pltpu.get_barrier_semaphore()
+    for dev in peers:
+        pl.semaphore_signal(barrier, inc=1, device_id=dev, device_id_type=MESH)
+    pl.semaphore_wait(barrier, len(peers))
+
+
+class RingGather:
+    def __init__(self, buf, cps, where, half):
+        xl, y, xh, z, c = where
+        self.buf, self.cps, self.half = buf, cps, half
+        self.g = gid(xl, y)
+        self.up = (self.g, tid(xh, z + 1, c))
+        self.down = (self.g, tid(xh, z + 3, c))
+        self.sib = (self.g, tid(xh, z, 1 - c))
+        self.me = z * 2 + c
+        self.zm = lax.rem(z + 3, 4) * 2 + c
+        self.zp = lax.rem(z + 1, 4) * 2 + c
+        self.far = lax.rem(z + 2, 4) * 2 + c
+
+    def begin(self):
+        own = self.buf.at[self.me]
+        self.cps.start(0, own, own, self.up)
+        self.cps.start(1, own, own, self.down)
+        self.cps.start(4, own, own, self.sib)
+
+    def middle(self):
+        (rl, cl), (rh, ch) = self.half
+        self.cps.arrived(0)
+        piece = self.buf.at[self.zm, rl, cl]
+        self.cps.start(2, piece, piece, self.up)
+        self.cps.arrived(1)
+        piece = self.buf.at[self.zp, rh, ch]
+        self.cps.start(3, piece, piece, self.down)
+        for k, zc in ((5, self.zm), (6, self.zp)):
+            self.cps.start(k, self.buf.at[zc], self.buf.at[zc], self.sib)
+
+    def last(self):
+        self.cps.arrived(2, 3)
+        self.cps.start(7, self.buf.at[self.far], self.buf.at[self.far], self.sib)
+
+    def end(self):
+        self.cps.arrived(4, 5, 6, 7)
+
+
+def front_kernel(
+    hidden, down, resid, grad, sel, hid_out, rows_out, cots_out,
+    hid, rows, cots, acc, sib_out, sib_in, z_out, z_in, x_out, x_in, pick_r, pick_c, resid_v, grad_v,
+    a_s, a_r, ca_s, ca_r, cg_s, cg_r, sb_s, sb_r, z_s, z_r, x_s, x_r, ra_s, ra_r, rg_s, rg_r, local_sem,
+):
+    where = place()
+    xl, y, xh, z, c = where
+    g, t = gid(xl, y), tid(xh, z, c)
+    me = z * 2 + c
+    width = resid.shape[1]
+    half_tok = 64
+
+    loads = [
+        pltpu.make_async_copy(hidden, hid.at[g], local_sem.at[0]),
+        pltpu.make_async_copy(resid, resid_v, local_sem.at[1]),
+        pltpu.make_async_copy(grad, grad_v, local_sem.at[2]),
+    ]
+    for cp in loads:
+        cp.start()
+
+    xp = (gid(1 - xl, y), t)
+    yp, ym = (gid(xl, y + 1), t), (gid(xl, y + 3), t)
+    sib = (g, tid(xh, z, 1 - c))
+    xhp = (g, tid(1 - xh, z, c))
+    group_peers = [(lax.rem(g + k, GROUPS), t) for k in range(1, GROUPS)]
+    z_peers = [(g, tid(xh, z + k, c)) for k in range(1, 4)]
+    enter(group_peers + z_peers + [sib, xhp])
+
+    for cp in loads:
+        cp.wait()
+
+    a = Copies(a_s, a_r)
+    ca = Copies(ca_s, ca_r)
+    cg = Copies(cg_s, cg_r)
+    sb = Copies(sb_s, sb_r)
+    xx = Copies(x_s, x_r)
+    ra = Copies(ra_s, ra_r)
+    rg = Copies(rg_s, rg_r)
+
+    a.start(0, hid.at[g], hid.at[g], xp)
+    a.start(1, hid.at[g], hid.at[g], yp)
+    a.start(2, hid.at[g], hid.at[g], ym)
+
+    cols = pl.ds(pl.multiple_of(g * width, 128), width)
+
+    def deal(copies, picked, buf, values):
+        picked[...] = jnp.dot(sel[...], values, preferred_element_type=F32).astype(BF16).reshape(picked.shape)
+        for k in range(1, GROUPS):
+            to = lax.rem(g + k, GROUPS)
+            copies.start(k - 1, picked.at[to // 2], buf.at[me, :, cols], (to, t))
+        buf[me, :, cols] = picked[g // 2]
+
+    deal(ca, pick_c, cots, grad_v[...])
+
+    row_halves = (
+        (slice(None), pl.ds(0, rows.shape[2] // 2)),
+        (slice(None), pl.ds(rows.shape[2] // 2, rows.shape[2] // 2)),
+    )
+    cot_ring = RingGather(cots, cg, where, row_halves)
+    row_ring = RingGather(rows, rg, where, row_halves)
+
+    order = [
+        (xl, y), (1 - xl, y), (xl, lax.rem(y + 3, 4)), (xl, lax.rem(y + 1, 4)), (xl, lax.rem(y + 2, 4)),
+        (1 - xl, lax.rem(y + 3, 4)), (1 - xl, lax.rem(y + 1, 4)), (1 - xl, lax.rem(y + 2, 4)),
+    ]
+
+    def multiply(k):
+        sx, sy = order[k]
+        acc[k] = jnp.dot(hid[gid(sx, sy)], down[...], preferred_element_type=F32).reshape(2, half_tok, width)
+        sib_out[k] = acc[k, 1 - c].astype(BF16)
+        sb.start(k, sib_out.at[k], sib_in.at[k], sib)
+
+    def z_copy(k):
+        sx, sy = order[k]
+        return pltpu.make_async_remote_copy(
+            src_ref=z_out.at[k], dst_ref=z_in.at[sx, z], send_sem=z_s.at[k], recv_sem=z_r.at[sx, z],
+            device_id=(g, tid(xh, sy, c)), device_id_type=MESH,
+        )
+
+    def pass_on(k):
+        sx, sy = order[k]
+        sb.arrived(k)
+        z_out[k] = (acc[k, c] + sib_in[k].astype(F32)).astype(BF16)
+
+        @pl.when(sy != z)
+        def _():
+            z_copy(k).start()
+
+        @pl.when(sy == z)
+        def _():
+            z_in[sx, z] = z_out[k]
+
+    multiply(0)
+    a.arrived(1)
+    piece = hid.at[gid(xl, y + 3), pl.ds(0, half_tok)]
+    a.start(3, piece, piece, yp)
+    a.arrived(2)
+    piece = hid.at[gid(xl, y + 1), pl.ds(half_tok, half_tok)]
+    a.start(4, piece, piece, ym)
+    a.arrived(0)
+    piece = hid.at[gid(1 - xl, y)]
+    a.start(5, piece, piece, yp)
+    a.start(6, piece, piece, ym)
+    ca.arrived(*range(GROUPS - 1))
+    cot_ring.begin()
+    multiply(1)
+    pass_on(0)
+    multiply(2)
+    pass_on(1)
+    multiply(3)
+    pass_on(2)
+    a.arrived(3, 4)
+    piece = hid.at[gid(xl, y + 2)]
+    a.start(7, piece, piece, xp)
+    multiply(4)
+    pass_on(3)
+    cot_ring.middle()
+    pass_on(4)
+    a.arrived(5)
+    multiply(5)
+    a.arrived(6)
+    multiply(6)
+    pass_on(5)
+    pass_on(6)
+    a.arrived(7)
+    multiply(7)
+    pass_on(7)
+    hid_cp = pltpu.make_async_copy(hid, hid_out, local_sem.at[0])
+    hid_cp.start()
+
+    for sx in range(2):
+        for dz in range(1, 4):
+            src = lax.rem(z + dz, 4)
+            pltpu.make_async_remote_copy(
+                src_ref=z_out.at[0], dst_ref=z_in.at[sx, src], send_sem=z_s.at[0], recv_sem=z_r.at[sx, src],
+                device_id=(g, tid(xh, z + dz, c)), device_id_type=MESH,
+            ).wait_recv()
+    parts = z_in[...].astype(F32)
+    x_out[...] = ((parts[:, 0] + parts[:, 1]) + (parts[:, 2] + parts[:, 3])).astype(BF16)
+    xx.start(0, x_out, x_in, xhp)
+    cot_ring.last()
+    xx.arrived(0)
+    total = (x_out[...].astype(F32) + x_in[...].astype(F32)).reshape(2 * half_tok, width)
+    stream = (resid_v[...].astype(F32) + total).astype(BF16)
+    deal(ra, pick_r, rows, stream)
+    ra.arrived(*range(GROUPS - 1))
+    row_ring.begin()
+    cot_ring.end()
+    cot_cp = pltpu.make_async_copy(cots, cots_out, local_sem.at[1])
+    cot_cp.start()
+    row_ring.middle()
+    row_ring.last()
+    row_ring.end()
+    row_cp = pltpu.make_async_copy(rows, rows_out, local_sem.at[2])
+    row_cp.start()
+
+    for cps in (a, ca, cg, sb, xx, ra, rg):
+        cps.finish()
+    for k in range(GROUPS):
+        @pl.when(order[k][1] != z)
+        def _():
+            z_copy(k).wait_send()
+    hid_cp.wait()
+    cot_cp.wait()
+    row_cp.wait()
+
+
+def front(hidden, down, resid, grad, sel):
+    tokens, inner = hidden.shape
+    width = down.shape[1]
+    slots = sel.shape[0] // 4
+    model = width * GROUPS
+    any_spec = pl.BlockSpec(memory_space=pl.ANY)
+    vmem = pl.BlockSpec(memory_space=pltpu.VMEM)
+    dma = pltpu.SemaphoreType.DMA
+    sems = []
+    for n in (8, 7, 8, 8):
+        sems += [dma((n,)), dma((n,))]
+    sems += [dma((8,)), dma((2, 4)), dma((1,)), dma((1,)), dma((7,)), dma((7,)), dma((8,)), dma((8,)), dma((3,))]
+    return pl.pallas_call(
+        front_kernel,
+        out_shape=(
+            jax.ShapeDtypeStruct((GROUPS, tokens, inner), BF16),
+            jax.ShapeDtypeStruct((ZC, slots, model), BF16),
+            jax.ShapeDtypeStruct((ZC, slots, model), BF16),
+        ),
+        in_specs=[any_spec, vmem, any_spec, any_spec, vmem],
+        out_specs=(any_spec, any_spec, any_spec),
+        scratch_shapes=[
+            pltpu.VMEM((GROUPS, tokens, inner), BF16),
+            pltpu.VMEM((ZC, slots, model), BF16),
+            pltpu.VMEM((ZC, slots, model), BF16),
+            pltpu.VMEM((8, 2, 64, width), F32),
+            pltpu.VMEM((8, 64, width), BF16),
+            pltpu.VMEM((8, 64, width), BF16),
+            pltpu.VMEM((8, 64, width), BF16),
+            pltpu.VMEM((2, 4, 64, width), BF16),
+            pltpu.VMEM((2, 64, width), BF16),
+            pltpu.VMEM((2, 64, width), BF16),
+            pltpu.VMEM((4, slots, width), BF16),
+            pltpu.VMEM((4, slots, width), BF16),
+            pltpu.VMEM((128, width), BF16),
+            pltpu.VMEM((128, width), BF16),
+        ] + sems,
+        compiler_params=pltpu.CompilerParams(
+            collective_id=0, has_side_effects=True, vmem_limit_bytes=56 * 1024 * 1024
+        ),
+        name="front",
+    )(hidden, down, resid, grad, sel)
 
 
 def norm_backward(d_normed, rows_f, inv_rms, scale_row, model_width):
@@ -16,41 +315,33 @@
     model_width = gain.shape[1]
     pair_size = groups // head_count
     dataset = lax.axis_index("group") // pair_size
+    zc = lax.rem(lax.axis_index("tensor"), 8)
     blocks = route.shape[0]
     slot_count = route.shape[2]
     tokens = residual.shape[0]
     block_len = tokens // blocks
     slice_width = residual.shape[1]
-    hidden_all = lax.all_gather(backbone_hidden, "group", axis=0, tiled=True)
-    partial_value = jnp.dot(hidden_all, backbone_down, preferred_element_type=jnp.float32)
-    summed = lax.psum(partial_value, "tensor")
-    stream = (residual.astype(jnp.float32) + summed).astype(jnp.bfloat16)
+
+    def mine(a):
+        pair = a.reshape((2, 8) + a.shape[1:])
+        return lax.dynamic_index_in_dim(pair, zc, 1, keepdims=False)
+
+    own_route = mine(route)
+    resid = mine(residual.reshape(blocks, block_len, slice_width)).reshape(2 * block_len, slice_width)
+    grad = mine(head_grad.reshape(blocks, block_len, slice_width)).reshape(2 * block_len, slice_width)
+    wanted = jnp.where(own_route >= 0, own_route + (jnp.arange(2, dtype=jnp.int32) * block_len)[:, None, None], -1)
+    wanted = wanted.transpose(1, 0, 2).reshape(head_count * 2 * slot_count)
+    sel = (wanted[:, None] == jnp.arange(2 * block_len, dtype=jnp.int32)[None]).astype(BF16)
+
+    hidden_all, rows8, cots8 = front(backbone_hidden, backbone_down, resid, grad, sel)
+    hidden_all = hidden_all.reshape(tokens, -1)
+
+    def by_block(a):
+        return a.reshape(8, 2, slot_count, model_width).transpose(1, 0, 2, 3).reshape(blocks * slot_count, model_width)
+
+    head_rows, cot_rows = by_block(rows8), by_block(cots8)
     places = lax.broadcasted_iota(jnp.int32, (blocks, head_count, slot_count, block_len), 3)
     dataset_selector = route[:, :, :, None] == places
-    select_low = dataset_selector.astype(jnp.bfloat16)
-    picked_rows = jnp.einsum(
-        "yija,yac->iyjc",
-        select_low,
-        stream.reshape(blocks, block_len, slice_width),
-        preferred_element_type=jnp.float32,
-    ).astype(jnp.bfloat16)
-    picked_cots = jnp.einsum(
-        "yija,yac->iyjc",
-        select_low,
-        head_grad.reshape(blocks, block_len, slice_width),
-        preferred_element_type=jnp.float32,
-    ).astype(jnp.bfloat16)
-
-    def outgoing(picked):
-        per_head = picked.reshape(head_count, blocks * slot_count, slice_width)
-        return jnp.repeat(per_head, pair_size, axis=0).reshape(
-            groups * blocks * slot_count, slice_width
-        )
-
-    head_rows, cot_rows = (
-        lax.all_to_all(outgoing(picked_rows), "group", split_axis=0, concat_axis=1, tiled=True),
-        lax.all_to_all(outgoing(picked_cots), "group", split_axis=0, concat_axis=1, tiled=True),
-    )
     rows_f = head_rows.astype(jnp.float32)
     inv_rms = lax.rsqrt(jnp.mean(rows_f * rows_f, axis=-1, keepdims=True) + 1e-06)
     scale_row = lax.dynamic_index_in_dim(gain, dataset, 0, keepdims=False)

time: 629 us -> 426 us (0.68)
  waiting for transfers between devices: 453 us -> 178 us
  Pallas kernels: 0 us -> 87.5 us
  matrix products: 48.6 us -> 37.2 us
  starting transfers between devices: 9.6 us -> 0.08 us
    psum x1 -> x0, waiting for transfers between devices: 150 us -> none  [local(): summed = lax.psum(partial_value, 'tensor')]
    pallas_call x0 -> x1, Pallas kernels: none -> 87.5 us  [front(): pl.pallas_call(front_kernel, out_shape=(jax.ShapeDtypeStruct((GROUPS, tok...]
    all_to_all x2 -> x0, waiting for transfers between devices: 72 us -> none  [the longest x1 39.6 us: local(): lax.all_to_all(outgoing(picked_rows), 'group', split_axis=0, concat_axis=...]
    all_gather x1 -> x0, waiting for transfers between devices: 56 us -> none  [local(): hidden_all = lax.all_gather(backbone_hidden, 'group', axis=0, tiled=True)]
    all_to_all x2 -> x0, starting transfers between devices: 9.26 us -> none  [the longest x1 4.7 us: local(): lax.all_to_all(outgoing(picked_rows), 'group', split_axis=0, concat_axis=...]
    dot_general x3 -> x0, matrix products: 8 us -> none  [the longest x1 6.56 us: local(): jnp.dot(hidden_all, backbone_down, preferred_element_type=jnp.float32)]
    convert_element_type x1 -> x3, other arithmetic: 1.99 us -> 9.42 us  [the longest x1 4.58 us: local(): normed = (rows_f * inv_rms * scale_row).astype(jnp.bfloat16)]
    unnamed x5 -> x3, waiting for transfers between devices: 27.4 us -> 30.2 us
  transfers between devices with their start and end apart: 6 -> 2, of which waited for: 6 -> 2; matrix products, arithmetic and copies ran while one was open for 6% -> 4% of each run, Pallas kernels for 0% -> 0%
where the time goes in v1:
time: 426 us; the launch traced here: 424 us
  waiting for transfers between devices  178 us (42%)
  Pallas kernels  87.5 us (21%)
  blocking collectives  48.1 us (11%)
  matrix products  37.2 us (9%)
  other arithmetic  33.1 us (8%)
  local copies, waits for them, and re-layouts  26 us (6%)
  between operations  14.3 us (3%)
    psum x1, waiting for transfers between devices, local(): lax.psum(d_normed.astype(jnp.bfloat16), 'tensor').astype(jnp.float32)  148 us
    pallas_call x1, Pallas kernels, front(): pl.pallas_call(front_kernel, out_shape=(jax.ShapeDtypeStruct((GROUPS, tok...  87.5 us
    all_to_all x1, blocking collectives, local(): lax.all_to_all(d_rows.astype(jnp.bfloat16), 'group', split_axis=1, concat...  48.1 us
    unnamed x3, waiting for transfers between devices  30.2 us
    unnamed x33, local copies, waits for them, and re-layouts  11.4 us
  transfers between devices with their start and end apart: 2, of which 2 were waited for; matrix products, arithmetic and copies ran while one was open for 4% of the time, Pallas kernels for 0%

profile of v1, /device:TPU:1, one launch (start us, length us, event | category | flops | bytes accessed | tf_op | source)
XLA Modules:
  0.0 424.1 jit_solution(3361458606560290430)
XLA Ops:
  7.2 0.0 copy-start
  7.2 0.0 all-reduce.2.cloned.1.call-start
  7.3 0.7 constant_dynamic-slice_fusion.1
  7.9 0.1 fusion.14
  8.0 0.1 eq.25
  8.1 0.7 fusion.13.sel
  8.8 2.0 copy.32.hidden
  10.8 1.7 constant_dynamic-slice_fusion.2
  12.6 87.5 %front.1 = (bf16[8,128,1728]{2,1,0:T(8,128)(2,1)}, bf16[8,48,5120]{2,1,0:T(8,128)(2,1)}, bf16[8,48,5120]{2,1,0:T(8,128)(2,1)}) custom-call(bf16[128,1728]{1,0:T(8,128)(2,1)} %copy.32.hidden, bf16[1728,640]{1,0:T(8,128)(2,1)} %down.1, bf16[128,640]{1,0:T(8,128)(2,1)} %bitcast.81, bf16[128,640]{1,0:T(8,128)(2,1)} %bitcast.80, bf16[192,128]{1,0:T(8,128)(2,1)} %fusion.13.sel), custom_call_target="tpu_custom_call" | custom-call | tf_op jit(solution)/shard_map/front/pallas_call | solution.py:274
  100.1 3.1 multiply_reduce_fusion
  103.2 0.2 copy-done.3
  103.4 4.1 convert_element_type.69
  107.5 4.3 %copy.34 = bf16[8,2,24,5120]{3,2,0,1:T(8,128)(2,1)} copy(bf16[8,2,24,5120]{3,2,1,0:T(8,128)(2,1)} %bitcast.78) | data formatting | bytes 7864320 | tf_op jit(solution)/shard_map/reshape | solution.py:340
  111.8 0.1 reshape.95
  111.9 0.1 rsqrt.15
  112.0 7.2 %copy.35 = f32[2,8,24,5120]{3,2,1,0:T(8,128)} copy(f32[2,8,24,5120]{3,2,0,1:T(8,128)} %bitcast.70) | data formatting | bytes 15728640 | tf_op jit(solution)/shard_map/convert_element_type | solution.py:345
  119.2 0.0 slice-start.2
  119.2 4.6 %fusion.1 = bf16[384,5120]{1,0:T(8,128)(2,1)S(1)} fusion(f32[2,8,24,5120]{3,2,1,0:T(8,128)} %copy.35, f32[5120]{0:T(1024)S(1)} %bitcast.82, f32[384]{0:T(512)S(1)} %rsqrt.15), kind=kLoop, calls=%fused_computation.4 | loop fusion | flops 5898240 | bytes 11818496 | tf_op jit(solution)/shard_map/convert_element_type | solution.py:348
  123.8 0.0 copy-start.6
  123.8 0.0 copy-start.4
  123.8 0.0 slice-start.3
  123.9 0.0 slice-start
  123.9 6.2 %fusion.16 = f32[384,432]{0,1:T(8,128)S(1)} fusion(bf16[384,5120]{1,0:T(8,128)(2,1)S(1)} %fusion.1, bf16[5120,432]{0,1:T(8,128)(2,1)} %param.13), kind=kOutput, calls=%fused_computation.43 | convolution fusion | flops 1698693120 | bytes 9019392 | tf_op jit(solution)/shard_map/dot_general | solution.py:349
  130.1 0.0 slice-start.1
  130.1 2.5 fusion.10
  132.7 4.2 convolution_convert_fusion.2
  136.8 0.0 all-reduce.2.cloned.1.call-update
  136.9 0.0 reduce-scatter.4.cloned.1.call-start
  136.9 147.5 %all-reduce.2.cloned.1.call-done = bf16[384,5120]{1,0:T(8,128)(2,1)} async-done(((bf16[384,5120]{1,0:T(8,128)(2,1)}), bf16[384,5120]{1,0:T(8,128)(2,1)}) %all-reduce.2.cloned.1.call-update) | async-done | bytes 3932176 | tf_op jit(solution)/shard_map/psum | solution.py:365
  284.4 5.6 %fusion.5 = f32[384]{0:T(512)S(1)} fusion(f32[2,8,24,5120]{3,2,1,0:T(8,128)} %copy.35, bf16[384,5120]{1,0:T(8,128)(2,1)} %all-reduce.2.cloned.1.call-done, f32[5120]{0:T(1024)S(1)} %bitcast.83), kind=kLoop, calls=%fused_computation.8 | loop fusion | flops 7863936 | bytes 11818496 | tf_op jit(solution)/shard_map/reduce_sum | solution.py:308
  290.1 5.0 %fusion.4 = bf16[384,5120]{1,0:T(8,128)(2,1)S(1)} fusion(f32[2,8,24,5120]{3,2,1,0:T(8,128)} %copy.35, bf16[384,5120]{1,0:T(8,128)(2,1)S(1)} %copy-done.2, f32[384]{0:T(512)S(1)} %broadcast_multiply_fusion, f32[384]{0:T(512)S(1)} %multiply_multiply_fusion, f32[5120]{0:T(1024)S(1)} %bitcast.84, f32[384]{0:T(512)S(1)} %rsqrt.15), kind=kLoop, calls=%fused_computation.7 | loop fusion | flops 13762560 | bytes 15753728 | tf_op jit(solution)/shard_map/convert_element_type | solution.py:368
  295.0 0.4 copy.51
  295.4 48.1 %all_to_all.13 = bf16[384,8,640]{2,0,1:T(8,128)(2,1)S(1)} all-to-all(bf16[384,8,640]{2,0,1:T(8,128)(2,1)S(1)} %bitcast.73), channel_id=1, replica_groups=mesh['group'=8,'tensor'=16] {'group'}, dimensions={1} | all-to-all | bytes 7864320 | tf_op jit(solution)/shard_map/all_to_all | solution.py:367
  343.5 3.6 convert_element_type.91
  347.1 6.1 %reduce_sum.32 = f32[4,16,24,640]{3,2,1,0:T(8,128)} reduce(f32[4,2,16,24,640]{4,3,2,1,0:T(8,128)} %bitcast.71, f32[]{:T(128)} %constant.49.clone.1), dimensions={1}, to_apply=%region_3.4 | reduce | flops 983040 | bytes 11796484 | tf_op jit(solution)/shard_map/reduce_sum | solution.py:372
  353.2 4.3 %fusion.6 = f32[16,64,640,1]{2,1,3,0:T(8,128)S(1)} fusion(f32[4,16,24,640]{3,2,1,0:T(8,128)} %reduce_sum.32, s32[16,4,24]{2,1,0:T(4,128)S(1)} %copy-done.9), kind=kOutput, calls=%fused_computation.15 | convolution fusion | flops 755073024 | bytes 6559744 | tf_op jit(solution)/shard_map/lret,rlez->ltz/dot_general | solution.py:373
  357.5 0.0 copy-start.7
  357.5 0.3 fusion.8
  357.8 1.3 copy-done.7
  359.1 4.4 %convolution_convert_fusion.3 = bf16[1024,1728]{0,1:T(8,128)(2,1)} fusion(bf16[1024,640]{1,0:T(8,128)(2,1)S(1)} %fusion.8, bf16[1728,640]{1,0:T(8,128)(2,1)S(1)} %copy-done.7), kind=kOutput, calls=%fused_computation.17 | convolution fusion | flops 2266693632 | bytes 7061504 | tf_op jit(solution)/shard_map/dot_general | solution.py:386
  363.5 5.9 %copy.40 = bf16[1024,1728]{1,0:T(8,128)(2,1)} copy(bf16[1024,1728]{0,1:T(8,128)(2,1)} %convolution_convert_fusion.3) | data formatting | bytes 7077888
  369.3 0.0 reduce-scatter.4.cloned.1.call-update
  369.4 0.0 copy-start.5
  369.4 6.8 %convolution_convert_fusion = bf16[5120,432]{0,1:T(8,128)(2,1)} fusion(bf16[384,432]{0,1:T(8,128)(2,1)S(1)} %fusion.10, bf16[384,5120]{1,0:T(8,128)(2,1)} %copy-done.6), kind=kOutput, calls=%fused_computation.11 | convolution fusion | flops 1700904960 | bytes 8687616 | tf_op jit(solution)/shard_map/dot_general | solution.py:359
  376.2 4.6 %convolution_convert_fusion.1 = bf16[432,5120]{1,0:T(8,128)(2,1)} fusion(bf16[384,5120]{1,0:T(8,128)(2,1)S(1)} %bitcast.77, f32[384,432]{0,1:T(8,128)S(1)} %fusion.16), kind=kOutput, calls=%fused_computation.12 | convolution fusion | flops 1701734400 | bytes 9019392 | tf_op jit(solution)/shard_map/dot_general | solution.py:356
  380.8 4.3 %convolution_convert_fusion.4 = bf16[1728,640]{1,0:T(8,128)(2,1)} fusion(bf16[1024,1728]{1,0:T(8,128)(2,1)S(1)} %bitcast.90, bf16[1024,640]{1,0:T(8,128)(2,1)S(1)} %fusion.8), kind=kOutput, calls=%fused_computation.18 | convolution fusion | flops 2266030080 | bytes 7061504 | tf_op jit(solution)/shard_map/dot_general | solution.py:382
  385.1 30.2 %reduce-scatter.4.cloned.1.call-done = bf16[128,1728]{1,0:T(8,128)(2,1)} async-done(((bf16[1024,1728]{1,0:T(8,128)(2,1)}), bf16[128,1728]{1,0:T(8,128)(2,1)}) %reduce-scatter.4.cloned.1.call-update) | async-done | bytes 442384
  415.3 2.0 copy.41
  (27 shorter events, 0.1 us)
Async XLA Ops:
  7.2 112.0 %copy-start = (f32[4,5120]{1,0:T(4,128)S(1)}, f32[4,5120]{1,0:T(4,128)}, u32[]{:S(2)}) copy-start(f32[4,5120]{1,0:T(4,128)} %param.12) | copy-start | bytes 245764
  7.2 277.3 %all-reduce.2.cloned.1.call-start = ((), (), s32[]{:S(2)}) async-start(), calls=%async_computation.2 | async-start | bytes 7864320 | tf_op jit(solution)/shard_map/psum | solution.py:365
  100.1 3.3 copy-start.3
  119.2 10.9 %slice-start.2 = ((s8[4423680]{0:T(1024)(128)(4,1)}), s8[4194304]{0:T(1024)(128)(4,1)S(1)}, s32[]{:S(2)}) async-start(s8[4423680]{0:T(1024)(128)(4,1)} %bitcast.88), calls=%async_computation.6 | async-start | bytes 8388608
  123.8 6.2 %copy-start.6 = (bf16[384,5120]{1,0:T(8,128)(2,1)}, bf16[384,5120]{1,0:T(8,128)(2,1)S(1)}, u32[]{:S(2)}) copy-start(bf16[384,5120]{1,0:T(8,128)(2,1)S(1)} %fusion.1) | copy-start | bytes 11796484
  123.8 6.2 %copy-start.4 = (bf16[8,2,24,5120]{3,2,0,1:T(8,128)(2,1)S(1)}, bf16[8,2,24,5120]{3,2,0,1:T(8,128)(2,1)}, u32[]{:S(2)}) copy-start(bf16[8,2,24,5120]{3,2,0,1:T(8,128)(2,1)} %copy.34) | copy-start | bytes 11796484
  123.8 6.2 %slice-start.3 = ((s8[4423680]{0:T(1024)(128)(4,1)}), s8[229376]{0:T(1024)(128)(4,1)S(1)}, s32[]{:S(2)}) async-start(s8[4423680]{0:T(1024)(128)(4,1)} %bitcast.88), calls=%async_computation.7 | async-start | bytes 458752
  123.9 8.8 %slice-start = ((s8[4423680]{0:T(1024)(128)(4,1)}), s8[4194304]{0:T(1024)(128)(4,1)S(1)}, s32[]{:S(2)}) async-start(s8[4423680]{0:T(1024)(128)(4,1)} %bitcast.74), calls=%async_computation.4 | async-start | bytes 8388608
  130.1 2.5 slice-start.1
  136.9 278.4 %reduce-scatter.4.cloned.1.call-start = ((), (), s32[]{:S(2)}) async-start(), calls=%async_computation.3 | async-start | bytes 4128768
  284.4 5.6 %copy-start.2 = (bf16[384,5120]{1,0:T(8,128)(2,1)S(1)}, bf16[384,5120]{1,0:T(8,128)(2,1)}, u32[]{:S(2)}) copy-start(bf16[384,5120]{1,0:T(8,128)(2,1)} %all-reduce.2.cloned.1.call-done) | copy-start | bytes 11796484
  347.1 6.1 %copy-start.9 = (s32[16,4,24]{2,1,0:T(4,128)S(1)}, s32[16,4,24]{2,1,0:T(4,128)}, u32[]{:S(2)}) copy-start(s32[16,4,24]{2,1,0:T(4,128)} %param.15) | copy-start | bytes 18436
  353.2 4.3 %copy-start.8 = (bf16[1024,640]{1,0:T(8,128)(2,1)S(1)}, bf16[1024,640]{1,0:T(8,128)(2,1)}, u32[]{:S(2)}) copy-start(bf16[1024,640]{1,0:T(8,128)(2,1)} %param.11) | copy-start | bytes 3932164
  357.5 1.6 copy-start.7
  369.4 6.8 %copy-start.5 = (bf16[8,2,24,5120]{3,2,0,1:T(8,128)(2,1)S(1)}, bf16[8,2,24,5120]{3,2,0,1:T(8,128)(2,1)}, u32[]{:S(2)}) copy-start(bf16[8,2,24,5120]{3,2,0,1:T(8,128)(2,1)} %copy.34) | copy-start | bytes 11796484
  376.2 4.6 %copy-start.10 = (bf16[8,128,1728]{2,1,0:T(8,128)(2,1)S(1)}, bf16[8,128,1728]{2,1,0:T(8,128)(2,1)}, u32[]{:S(2)}) copy-start(bf16[8,128,1728]{2,1,0:T(8,128)(2,1)} %get-tuple-element.9) | copy-start | bytes 10616836
  380.8 36.5 %copy-start.1 = (f32[4,5120]{1,0:T(4,128)S(1)}, f32[4,5120]{1,0:T(4,128)}, u32[]{:S(2)}) copy-start(f32[4,5120]{1,0:T(4,128)} %param.12) | copy-start | bytes 245764
Sparse Core Ops, SparseCore 0:
  137.0 147.4 all-reduce.1
  369.5 45.7 reduce-scatter.3

commit v2 on v1

v2 whole, which is shorter than its diff:
```python
import jax
import jax.numpy as jnp
from jax import lax
from jax.experimental import pallas as pl
from jax.experimental.pallas import tpu as pltpu
from jax.sharding import PartitionSpec as P

MESH = pl.DeviceIdType.MESH
F32 = jnp.float32
BF16 = jnp.bfloat16
GROUPS = 8
ZC = 8


def place():
    g = lax.axis_index("group")
    t = lax.axis_index("tensor")
    return g // 4, g % 4, t // 8, (t // 2) % 4, t % 2


def gid(xl, y):
    return xl * 4 + lax.rem(y, 4)


def tid(xh, z, c):
    return xh * 8 + lax.rem(z, 4) * 2 + c


class Copies:
    def __init__(self, send, recv):
        self.send, self.recv, self.made = send, recv, {}

    def start(self, k, src, dst, dev):
        cp = pltpu.make_async_remote_copy(
            src_ref=src, dst_ref=dst, send_sem=self.send.at[k], recv_sem=self.recv.at[k],
            device_id=dev, device_id_type=MESH,
        )
        cp.start()
        self.made[k] = cp

    def arrived(self, *ks):
        for k in ks:
            self.made[k].wait_recv()

    def finish(self):
        for cp in self.made.values():
            cp.wait_send()


def enter(peers):
    barrier = pltpu.get_barrier_semaphore()
    for dev in peers:
        pl.semaphore_signal(barrier, inc=1, device_id=dev, device_id_type=MESH)
    pl.semaphore_wait(barrier, len(peers))


class RingGather:
    def __init__(self, buf, cps, where, half):
        xl, y, xh, z, c = where
        self.buf, self.cps, self.half = buf, cps, half
        self.g = gid(xl, y)
        self.up = (self.g, tid(xh, z + 1, c))
        self.down = (self.g, tid(xh, z + 3, c))
        self.sib = (self.g, tid(xh, z, 1 - c))
        self.me = z * 2 + c
        self.zm = lax.rem(z + 3, 4) * 2 + c
        self.zp = lax.rem(z + 1, 4) * 2 + c
        self.far = lax.rem(z + 2, 4) * 2 + c

    def begin(self):
        own = self.buf.at[self.me]
        self.cps.start(0, own, own, self.up)
        self.cps.start(1, own, own, self.down)
        self.cps.start(4, own, own, self.sib)

    def middle(self):
        (rl, cl), (rh, ch) = self.half
        self.cps.arrived(0)
        piece = self.buf.at[self.zm, rl, cl]
        self.cps.start(2, piece, piece, self.up)
        self.cps.arrived(1)
        piece = self.buf.at[self.zp, rh, ch]
        self.cps.start(3, piece, piece, self.down)
        for k, zc in ((5, self.zm), (6, self.zp)):
            self.cps.start(k, self.buf.at[zc], self.buf.at[zc], self.sib)

    def last(self):
        self.cps.arrived(2, 3)
        self.cps.start(7, self.buf.at[self.far], self.buf.at[self.far], self.sib)

    def end(self):
        self.cps.arrived(4, 5, 6, 7)

NT = (((1,), (1,)), ((), ()))
TN = (((0,), (0,)), ((), ()))


def kernel(
    hidden_t, down_h, resid, grad, gain, w_up_t, w_down, sel, sel_back,
    gh_out, gb_out, gu_out, gd_out,
    hid, down, wu, wd, rows, cots, normed,
    acc, sib_out, sib_in, z_out, z_in, x_out, x_in, pick_r, pick_c, resid_v, grad_v,
    pre, dact, act_t, dpre_t, dpre,
    stage, dn, sd_out, sd_in, far_out, far_in, dir_out, dir_in, sum_out, sum_in,
    tot, drow, back_in, x2_out, x2_in, ds, fp, fin, fhalf, gh_v,
    a_s, a_r, ca_s, ca_r, cg_s, cg_r, sb_s, sb_r, z_s, z_r, x_s, x_r, ra_s, ra_r, rg_s, rg_r,
    sd_s, sd_r, fr_s, fr_r, nd_s, nd_r, ns_s, ns_r, ba_s, ba_r, x2_s, x2_r, dg_s, dg_r, f_s, f_r, local_sem,
):
    where = place()
    xl, y, xh, z, c = where
    g, t = gid(xl, y), tid(xh, z, c)
    me = z * 2 + c
    head = g // 2
    width = resid.shape[1]
    model = rows.shape[2]
    inner = hid.shape[1]
    slots = rows.shape[1]
    part = inner // 2

    loads = [pltpu.make_async_copy(hidden_t, hid.at[g], local_sem.at[0])]
    for i in range(2):
        tok = pl.ds(pl.multiple_of((8 * i + me) * 64, 64), 64)
        loads.append(pltpu.make_async_copy(grad.at[tok], grad_v.at[pl.ds(64 * i, 64)], local_sem.at[1 + i]))
        loads.append(pltpu.make_async_copy(resid.at[tok], resid_v.at[pl.ds(64 * i, 64)], local_sem.at[3 + i]))
    late = [
        pltpu.make_async_copy(down_h, down, local_sem.at[5]),
        pltpu.make_async_copy(w_down, wd, local_sem.at[6]),
        pltpu.make_async_copy(w_up_t, wu, local_sem.at[7]),
    ]
    for cp in loads:
        cp.start()

    xp = (gid(1 - xl, y), t)
    yp, ym = (gid(xl, y + 1), t), (gid(xl, y + 3), t)
    sib = (g, tid(xh, z, 1 - c))
    xhp = (g, tid(1 - xh, z, c))
    zup, zdown = (g, tid(xh, z + 1, c)), (g, tid(xh, z + 3, c))
    group_peers = [(lax.rem(g + k, GROUPS), t) for k in range(1, GROUPS)]
    z_peers = [(g, tid(xh, z + k, c)) for k in range(1, 4)]
    with jax.named_scope("enter"):
        enter(group_peers + z_peers + [sib, xhp])
        for cp in loads:
            cp.wait()

    a, ca, cg, sb = Copies(a_s, a_r), Copies(ca_s, ca_r), Copies(cg_s, cg_r), Copies(sb_s, sb_r)
    xx, ra, rg = Copies(x_s, x_r), Copies(ra_s, ra_r), Copies(rg_s, rg_r)
    sd, fr, nd, ns = Copies(sd_s, sd_r), Copies(fr_s, fr_r), Copies(nd_s, nd_r), Copies(ns_s, ns_r)
    ba, x2, dg, f = Copies(ba_s, ba_r), Copies(x2_s, x2_r), Copies(dg_s, dg_r), Copies(f_s, f_r)

    a.start(0, hid.at[g], hid.at[g], xp)
    a.start(1, hid.at[g], hid.at[g], yp)
    a.start(2, hid.at[g], hid.at[g], ym)
    for cp in late:
        cp.start()

    def cols(j):
        return pl.ds(pl.multiple_of(j * width, 128), width)

    def deal(copies, picked, buf, values):
        picked[...] = jnp.dot(sel[...], values, preferred_element_type=F32).astype(BF16).reshape(picked.shape)
        for k in range(1, GROUPS):
            to = lax.rem(g + k, GROUPS)
            copies.start(k - 1, picked.at[to // 2], buf.at[me, :, cols(g)], (to, t))
        buf[me, :, cols(g)] = picked[head]

    deal(ca, pick_c, cots, grad_v[...])

    row_halves = (
        (slice(None), pl.ds(0, model // 2)),
        (slice(None), pl.ds(model // 2, model // 2)),
    )
    tok_halves = ((pl.ds(0, 64), slice(None)), (pl.ds(64, 64), slice(None)))
    cot_ring = RingGather(cots, cg, where, row_halves)
    row_ring = RingGather(rows, rg, where, row_halves)
    ds_ring = RingGather(ds, dg, where, tok_halves)

    order = [
        (xl, y), (1 - xl, y), (xl, lax.rem(y + 3, 4)), (xl, lax.rem(y + 1, 4)), (xl, lax.rem(y + 2, 4)),
        (1 - xl, lax.rem(y + 3, 4)), (1 - xl, lax.rem(y + 1, 4)), (1 - xl, lax.rem(y + 2, 4)),
    ]

    def multiply(k):
        sx, sy = order[k]
        acc[k] = lax.dot_general(hid[gid(sx, sy)], down[...], TN, preferred_element_type=F32).reshape(2, 64, width)
        sib_out[k] = acc[k, 1 - c].astype(BF16)
        sb.start(k, sib_out.at[k], sib_in.at[k], sib)

    def z_copy(k):
        sx, sy = order[k]
        return pltpu.make_async_remote_copy(
            src_ref=z_out.at[k], dst_ref=z_in.at[sx, z], send_sem=z_s.at[k], recv_sem=z_r.at[sx, z],
            device_id=(g, tid(xh, sy, c)), device_id_type=MESH,
        )

    def pass_on(k):
        sx, sy = order[k]
        sb.arrived(k)
        z_out[k] = (acc[k, c] + sib_in[k].astype(F32)).astype(BF16)

        @pl.when(sy != z)
        def _():
            z_copy(k).start()

        @pl.when(sy == z)
        def _():
            z_in[sx, z] = z_out[k]

    k_step = 1024

    def product(total, weights, values, lo, hi):
        @pl.loop(lo, hi)
        def _(k):
            kc = pl.ds(pl.multiple_of(k * k_step, 128), k_step)
            term = lax.dot_general(
                weights[:, kc], values[:, :, kc].reshape(ZC * slots, k_step), NT, preferred_element_type=F32
            )
            total[...] += term

    with jax.named_scope("gather_hidden"):
        late[0].wait()
        multiply(0)
        a.arrived(1)
        piece = hid.at[gid(xl, y + 3), pl.ds(0, part)]
        a.start(3, piece, piece, yp)
        a.arrived(2)
        piece = hid.at[gid(xl, y + 1), pl.ds(part, part)]
        a.start(4, piece, piece, ym)
        a.arrived(0)
        piece = hid.at[gid(1 - xl, y)]
        a.start(5, piece, piece, yp)
        a.start(6, piece, piece, ym)
        ca.arrived(*range(GROUPS - 1))
        cot_ring.begin()
        multiply(1)
        pass_on(0)
        multiply(2)
        pass_on(1)
        multiply(3)
        pass_on(2)
        a.arrived(3, 4)
        piece = hid.at[gid(xl, y + 2)]
        a.start(7, piece, piece, xp)
        multiply(4)
        pass_on(3)
        pass_on(4)
    with jax.named_scope("gather_cots"):
        cot_ring.middle()
        pre[...] = jnp.zeros_like(pre)
        dact[...] = jnp.zeros_like(dact)
    with jax.named_scope("gather_rest"):
        a.arrived(5)
        multiply(5)
        a.arrived(6)
        multiply(6)
        pass_on(5)
        pass_on(6)
        a.arrived(7)
        multiply(7)
        pass_on(7)
    with jax.named_scope("sum_stream"):
        cot_ring.last()
        for sx in range(2):
            for dz in range(1, 4):
                src = lax.rem(z + dz, 4)
                pltpu.make_async_remote_copy(
                    src_ref=z_out.at[0], dst_ref=z_in.at[sx, src], send_sem=z_s.at[0], recv_sem=z_r.at[sx, src],
                    device_id=(g, tid(xh, z + dz, c)), device_id_type=MESH,
                ).wait_recv()
        parts = z_in[...].astype(F32)
        x_out[...] = ((parts[:, 0] + parts[:, 1]) + (parts[:, 2] + parts[:, 3])).astype(BF16)
        xx.start(0, x_out, x_in, xhp)
        xx.arrived(0)
        total = (x_out[...].astype(F32) + x_in[...].astype(F32)).reshape(2 * 64, width)
        stream = (resid_v[...].astype(F32) + total).astype(BF16)
    with jax.named_scope("deal_rows"):
        deal(ra, pick_r, rows, stream)
        ra.arrived(*range(GROUPS - 1))
        row_ring.begin()

    def gain_at(j):
        return gain[pl.ds(head, 1), cols(j)]

    def norm_shard(zc):
        def add(j, squares):
            v = rows[zc, :, cols(j)].astype(F32)
            return squares + v * v

        squares = lax.fori_loop(0, GROUPS, add, jnp.zeros((slots, width), F32))
        inv = lax.rsqrt(jnp.sum(squares, axis=-1, keepdims=True) * (1.0 / model) + 1e-06)

        @pl.loop(0, GROUPS)
        def _(j):
            v = rows[zc, :, cols(j)].astype(F32)
            normed[zc, :, cols(j)] = (v * inv * gain_at(j)).astype(BF16)

        return inv

    with jax.named_scope("gather_rows"):
        cot_ring.end()
        late[1].wait()
        late[2].wait()
        inv_own = norm_shard(me)
        product(dact, wd, cots, 0, 5)
        row_ring.middle()
        row_ring.cps.arrived(4)
        norm_shard(z * 2 + 1 - c)
        norm_shard(row_ring.zm)
        norm_shard(row_ring.zp)
        row_ring.cps.arrived(5, 6)
        norm_shard(lax.rem(z + 3, 4) * 2 + 1 - c)
        norm_shard(lax.rem(z + 1, 4) * 2 + 1 - c)
        row_ring.last()
        norm_shard(row_ring.far)
        row_ring.cps.arrived(7)
        norm_shard(lax.rem(z + 2, 4) * 2 + 1 - c)

    with jax.named_scope("heads"):
        product(pre, wu, normed, 0, 5)

        @pl.loop(0, pre.shape[0] // 48)
        def _(i):
            r = pl.ds(pl.multiple_of(i * 48, 16), 48)
            p = pre[r, :]
            s = jax.nn.sigmoid(p)
            act_t[r, :] = (p * s).astype(BF16)
            dpre_t[r, :] = (dact[r, :] * s * (1.0 + p * (1.0 - s))).astype(BF16)

        dpre[...] = dpre_t[...].T

    def dn_multiply(j):
        stage[...] = jnp.dot(dpre[...], wu[:, cols(j)], preferred_element_type=F32).reshape(stage.shape)
        dn[j] = stage[:, c]
        sd_out[j] = stage[:, 1 - c].astype(BF16)
        sd.start(j, sd_out.at[j], sd_in.at[j], sib)

    def toward(j):
        return (zup, zdown, lax.rem(z + 1, 4), lax.rem(z + 3, 4)) if j < 4 else (
            zdown, zup, lax.rem(z + 3, 4), lax.rem(z + 1, 4))

    def dn_split(j):
        to, other, z_to, z_other = toward(j)
        sd.arrived(j)
        dn[j] = dn[j] + sd_in[j].astype(F32)
        far_out[j] = dn[j, lax.rem(z + 2, 4)].astype(BF16)
        fr.start(j, far_out.at[j], far_in.at[j], to)
        dir_out[j] = dn[j, z_other].astype(BF16)
        nd.start(j, dir_out.at[j], dir_in.at[j], other)

    def dn_forward(j):
        to, other, z_to, z_other = toward(j)
        fr.arrived(j)
        sum_out[j] = (dn[j, z_to] + far_in[j].astype(F32)).astype(BF16)
        ns.start(j, sum_out.at[j], sum_in.at[j], to)

    js = [0, 4, 1, 5, 2, 6, 3, 7]
    with jax.named_scope("row_gradients"):
        for i in range(len(js) + 3):
            if i < 8:
                dn_multiply(js[i])
            if 0 <= i - 1 < 8:
                dn_split(js[i - 1])
            if 0 <= i - 3 < 8:
                dn_forward(js[i - 3])

    def down_grad(j):
        wd[:, cols(j)] = jnp.dot(
            act_t[...], cots[:, :, cols(j)].reshape(ZC * slots, width), preferred_element_type=F32
        ).astype(BF16)

    def up_grad(j):
        wu[:, cols(j)] = jnp.dot(
            dpre_t[...], normed[:, :, cols(j)].reshape(ZC * slots, width), preferred_element_type=F32
        ).astype(BF16)

    with jax.named_scope("down_grads"):
        pl.loop(0, GROUPS)(down_grad)
        gd_copy = pltpu.make_async_copy(wd, gd_out, local_sem.at[0])
        gd_copy.start()

    with jax.named_scope("norm_backward"):
        dot_sum = jnp.zeros((slots, width), F32)
        for j in js:
            ns.arrived(j)
            nd.arrived(j)
            q = (dn[j, z] + sum_in[j].astype(F32) + dir_in[j].astype(F32)) * gain_at(j)
            tot[j] = q
            dot_sum = dot_sum + q * rows[me, :, cols(j)].astype(F32)
        back = inv_own * inv_own * inv_own * (jnp.sum(dot_sum, axis=-1, keepdims=True) * (1.0 / model))

        @pl.loop(0, GROUPS)
        def _(j):
            drow[j] = (inv_own * tot[j] - rows[me, :, cols(j)].astype(F32) * back).astype(BF16)

        for k in range(1, GROUPS):
            to = lax.rem(g + k, GROUPS)
            ba.start(k - 1, drow.at[to], back_in.at[g], (to, t))
        back_in[g] = drow[g]

    with jax.named_scope("return_rows"):
        pl.loop(0, 3)(up_grad)
        ba.arrived(*range(GROUPS - 1))
        x2_out[...] = jnp.dot(
            sel_back[...], back_in[...].reshape(GROUPS * slots, width), preferred_element_type=F32
        ).astype(BF16)
        x2.start(0, x2_out, x2_in, xhp)
        x2.arrived(0)
        ds[me] = (grad_v[...].astype(F32) + (x2_out[...].astype(F32) + x2_in[...].astype(F32))).astype(BF16)
        ds_ring.begin()
    with jax.named_scope("gather_dstream"):
        pl.loop(3, GROUPS)(up_grad)
        gu_copy = pltpu.make_async_copy(wu, gu_out, local_sem.at[1])
        gu_copy.start()
        ds_ring.middle()
        ds_ring.last()
        ds_ring.end()

    def tokens_of(sx, sy):
        at = pl.ds(pl.multiple_of(sx * 64, 64), 64)
        return [ds[sy * 2, at, :], ds[sy * 2 + 1, at, :]]

    m_step = inner // 4

    def hidden_grads(i, first, second):
        both = jnp.concatenate(tokens_of(*first) + tokens_of(*second), axis=0)

        @pl.loop(0, 4)
        def _(m):
            r = pl.ds(pl.multiple_of(m * m_step, 16), m_step)
            p = lax.dot_general(down[r, :], both, NT, preferred_element_type=F32).astype(BF16)
            fp[i, r, :] = p[:, :128]
            fp[i + 1, r, :] = p[:, 128:]

    y1, y2, y3 = lax.rem(y + 1, 4), lax.rem(y + 2, 4), lax.rem(y + 3, 4)
    low, high = pl.ds(0, part), pl.ds(part, part)

    def add_into(dst, *terms):
        total = dst[...].astype(F32)
        for term in terms:
            total = total + term[...].astype(F32)
        return total.astype(BF16)

    with jax.named_scope("hidden_grads"):
        hidden_grads(2, (1 - xl, y1), (1 - xl, y3))
        f.start(0, fp.at[2], fin.at[0], yp)
        f.start(1, fp.at[3], fin.at[1], ym)
        hidden_grads(0, (1 - xl, y2), (xl, y2))
        f.start(2, fp.at[0], fin.at[2], xp)
        hidden_grads(4, (xl, y1), (xl, y3))
        f.start(3, fp.at[4, high], fin.at[3, high], yp)
        f.start(4, fp.at[5, low], fin.at[4, low], ym)
        hidden_grads(6, (1 - xl, y), (xl, y))

    def backbone_grad(m):
        r = pl.ds(pl.multiple_of(m * m_step, 16), m_step)
        total = jnp.zeros((m_step, width), F32)
        for i in range(4):
            left = jnp.concatenate([hid[2 * i, r, :], hid[2 * i + 1, r, :]], axis=1)
            right = jnp.concatenate(
                tokens_of((2 * i) // 4, (2 * i) % 4) + tokens_of((2 * i + 1) // 4, (2 * i + 1) % 4), axis=0)
            total = total + jnp.dot(left, right, preferred_element_type=F32)
        down[r, :] = total.astype(BF16)

    with jax.named_scope("sum_hidden_grads"):
        f.arrived(2)
        fp[1] = add_into(fp.at[1], fin.at[2])
        f.start(5, fp.at[1, low], fhalf.at[0], yp)
        f.start(6, fp.at[1, high], fhalf.at[1], ym)
        f.arrived(0, 1)
        fp[6] = add_into(fp.at[6], fin.at[0], fin.at[1])
        f.start(7, fp.at[6], fin.at[5], xp)
        pl.loop(0, 4)(backbone_grad)
        gb_copy = pltpu.make_async_copy(down, gb_out, local_sem.at[2])
        gb_copy.start()
        f.arrived(5)
        fp[4, low] = add_into(fp.at[4, low], fhalf.at[0])
        f.start(8, fp.at[4, low], fin.at[3, low], yp)
        f.arrived(6)
        fp[5, high] = add_into(fp.at[5, high], fhalf.at[1])
        f.start(9, fp.at[5, high], fin.at[4, high], ym)
        f.arrived(7)
        fp[7] = add_into(fp.at[7], fin.at[5])
        f.arrived(3, 4, 8, 9)
        gh_v[...] = add_into(fp.at[7], fin.at[3], fin.at[4])
        gh_copy = pltpu.make_async_copy(gh_v, gh_out, local_sem.at[3])
        gh_copy.start()

    with jax.named_scope("finish"):
        for cps in (a, ca, cg, sb, xx, ra, rg, sd, fr, nd, ns, ba, x2, dg, f):
            cps.finish()
        for k in range(GROUPS):
            @pl.when(order[k][1] != z)
            def _():
                z_copy(k).wait_send()
        for cp in (gd_copy, gu_copy, gb_copy, gh_copy):
            cp.wait()


def run(hidden_t, down, resid, grad, gain, w_up_t, w_down, sel, sel_back):
    inner, tokens = hidden_t.shape
    width = down.shape[1]
    slots = sel.shape[0] // 4
    model = width * GROUPS
    units = w_down.shape[0]
    any_spec = pl.BlockSpec(memory_space=pl.ANY)
    vmem = pl.BlockSpec(memory_space=pltpu.VMEM)
    dma = pltpu.SemaphoreType.DMA
    sems = []
    for n in ((8,), (7,), (8,), (8,)):
        sems += [dma(n), dma(n)]
    sems += [dma((8,)), dma((2, 4))]
    for n in ((1,), (7,), (8,), (8,), (8,), (8,), (8,), (7,), (1,), (8,), (10,)):
        sems += [dma(n), dma(n)]
    sems += [dma((8,))]
    piece = (64, width)
    return pl.pallas_call(
        kernel,
        out_shape=(
            jax.ShapeDtypeStruct((inner, tokens), BF16),
            jax.ShapeDtypeStruct((inner, width), BF16),
            jax.ShapeDtypeStruct((units, model), BF16),
            jax.ShapeDtypeStruct((units, model), BF16),
        ),
        in_specs=[any_spec] * 4 + [vmem] + [any_spec] * 2 + [vmem] * 2,
        out_specs=(any_spec,) * 4,
        scratch_shapes=[
            pltpu.VMEM((GROUPS, inner, tokens), BF16),
            pltpu.VMEM((inner, width), BF16),
            pltpu.VMEM((units, model), BF16),
            pltpu.VMEM((units, model), BF16),
            pltpu.VMEM((ZC, slots, model), BF16),
            pltpu.VMEM((ZC, slots, model), BF16),
            pltpu.VMEM((ZC, slots, model), BF16),
            pltpu.VMEM((8, 2) + piece, F32),
            pltpu.VMEM((8,) + piece, BF16),
            pltpu.VMEM((8,) + piece, BF16),
            pltpu.VMEM((8,) + piece, BF16),
            pltpu.VMEM((2, 4) + piece, BF16),
            pltpu.VMEM((2,) + piece, BF16),
            pltpu.VMEM((2,) + piece, BF16),
            pltpu.VMEM((4, slots, width), BF16),
            pltpu.VMEM((4, slots, width), BF16),
            pltpu.VMEM((128, width), BF16),
            pltpu.VMEM((128, width), BF16),
            pltpu.VMEM((units, ZC * slots), F32),
            pltpu.VMEM((units, ZC * slots), F32),
            pltpu.VMEM((units, ZC * slots), BF16),
            pltpu.VMEM((units, ZC * slots), BF16),
            pltpu.VMEM((ZC * slots, units), BF16),
            pltpu.VMEM((4, 2, slots, width), F32),
            pltpu.VMEM((8, 4, slots, width), F32),
            pltpu.VMEM((8, 4, slots, width), BF16),
            pltpu.VMEM((8, 4, slots, width), BF16),
        ]
        + [pltpu.VMEM((8, slots, width), BF16)] * 6
        + [
            pltpu.VMEM((8, slots, width), F32),
            pltpu.VMEM((8, slots, width), BF16),
            pltpu.VMEM((8, slots, width), BF16),
            pltpu.VMEM((128, width), BF16),
            pltpu.VMEM((128, width), BF16),
            pltpu.VMEM((8, 128, width), BF16),
            pltpu.VMEM((8, inner, tokens), BF16),
            pltpu.VMEM((6, inner, tokens), BF16),
            pltpu.VMEM((2, inner // 2, tokens), BF16),
            pltpu.VMEM((inner, tokens), BF16),
        ]
        + sems,
        compiler_params=pltpu.CompilerParams(
            collective_id=0, has_side_effects=True, vmem_limit_bytes=62 * 1024 * 1024
        ),
        name="backbone_and_heads",
    )(hidden_t, down, resid, grad, gain, w_up_t, w_down, sel, sel_back)


def local(backbone_hidden, backbone_down, residual, head_grad, gain, w_up, w_down, route):
    groups = lax.axis_size("group")
    heads = gain.shape[0]
    zc = lax.rem(lax.axis_index("tensor"), ZC)
    blocks, _, slot_count = route.shape
    block_len = residual.shape[0] // blocks
    own = lax.dynamic_index_in_dim(route.reshape(2, ZC, heads, slot_count), zc, 1, keepdims=False)
    wanted = jnp.where(own >= 0, own + (jnp.arange(2, dtype=jnp.int32) * block_len)[:, None, None], -1)
    wanted = wanted.transpose(1, 0, 2).reshape(heads, 2 * slot_count)
    positions = jnp.arange(2 * block_len, dtype=jnp.int32)
    sel = (wanted.reshape(-1)[:, None] == positions[None]).astype(BF16)
    twice = jnp.repeat(wanted, groups // heads, axis=0).reshape(-1)
    sel_back = (positions[:, None] == twice[None]).astype(BF16)
    gh, gb, gu, gd = run(
        backbone_hidden.T, backbone_down, residual, head_grad, gain, w_up.T, w_down, sel, sel_back
    )
    return (gh.T, gb, gu.T, gd)


def solution(mesh):
    placed = (
        P("group", "tensor"),
        P("tensor", "group"),
        P(None, "group"),
        P(None, "group"),
        P(),
        P(None, ("group", "tensor")),
        P(("group", "tensor"), None),
        P(),
    )
    return jax.shard_map(
        local,
        mesh=mesh,
        in_specs=placed,
        out_specs=(
            P("group", "tensor"),
            P("tensor", "group"),
            P(None, ("group", "tensor")),
            P(("group", "tensor"), None),
        ),
        check_vma=False,
    )
```

time: 426 us -> 181 us (0.42)
  waiting for transfers between devices: 178 us -> 0 us
  Pallas kernels: 87.5 us -> 168 us
  blocking collectives: 48.1 us -> 0 us
  matrix products: 37.2 us -> 0 us
  other arithmetic: 33.1 us -> 1.47 us
  local copies, waits for them, and re-layouts: 26 us -> 10.5 us
  between operations: 14.3 us -> 0.67 us
    psum x1 -> x0, waiting for transfers between devices: 148 us -> none  [local(): lax.psum(d_normed.astype(jnp.bfloat16), 'tensor').astype(jnp.float32)]
    pallas_call x1, Pallas kernels: 87.5 us -> 168 us  [run(): pl.pallas_call(kernel, out_shape=(jax.ShapeDtypeStruct((inner, tokens), B...]
    all_to_all x1 -> x0, blocking collectives: 48.1 us -> none  [local(): lax.all_to_all(d_rows.astype(jnp.bfloat16), 'group', split_axis=1, concat...]
    dot_general x8 -> x0, matrix products: 37.2 us -> none  [the longest x1 6.81 us: local(): lax.dot_general(normed, d_pre, (((0,), (0,)), ((), ())), preferred_elemen...]
    unnamed x3 -> x0, waiting for transfers between devices: 30.2 us -> none
    convert_element_type x6 -> x2, other arithmetic: 18.2 us -> 1.39 us  [the longest x1 0.73 us: local(): sel = (wanted.reshape(-1)[:, None] == positions[None]).astype(BF16)]
    reduce_sum x3 -> x0, other arithmetic: 14.8 us -> none  [the longest x1 6.07 us: local(): returned_rows = returned_rows.reshape(head_count, pair_size, blocks, slot...]
    convert_element_type x1 -> x0, local copies, waits for them, and re-layouts: 7.17 us -> none  [local(): rows_f = head_rows.astype(jnp.float32)]
  transfers between devices with their start and end apart: 2 -> 0, of which waited for: 2 -> 0; matrix products, arithmetic and copies ran while one was open for 4% -> 0% of each run, Pallas kernels for 0% -> 0%
where the time goes in v2:
time: 181 us
  Pallas kernels  168 us (93%)
  local copies, waits for them, and re-layouts  10.5 us (6%)
    pallas_call x1, Pallas kernels, run(): pl.pallas_call(kernel, out_shape=(jax.ShapeDtypeStruct((inner, tokens), B...  168 us
    unnamed x12, local copies, waits for them, and re-layouts  10.2 us

profile of v2, /device:TPU:1, one launch (start us, length us, event | category | flops | bytes accessed | tf_op | source)
XLA Modules:
  0.0 181.0 jit_solution(2139011518709878635)
XLA Ops:
  0.6 0.0 copy-start
  0.7 0.7 copy-done
  1.4 0.1 fusion.2
  1.5 0.1 eq.30
  1.6 0.1 reshape.21
  1.6 0.1 eq.35
  1.7 0.7 fusion.1.sel
  2.5 0.7 fusion.sel_back
  3.1 168.4 %backbone_and_heads.1 = (bf16[1728,128]{1,0:T(8,128)(2,1)}, bf16[1728,640]{1,0:T(8,128)(2,1)}, bf16[432,5120]{1,0:T(8,128)(2,1)}, bf16[432,5120]{1,0:T(8,128)(2,1)}) custom-call(bf16[1728,128]{1,0:T(8,128)(2,1)} %bitcast.17, bf16[1728,640]{1,0:T(8,128)(2,1)} %down_h.1, bf16[1024,640]{1,0:T(8,128)(2,1)} %resid.1, bf16[1024,640]{1,0:T(8,128)(2,1)} %grad.1, ...), custom_call_target="tpu_custom_call" | custom-call | tf_op jit(solution)/shard_map/backbone_and_heads/pallas_call | solution.py:515
  171.5 0.0 copy-start.1
  171.5 2.0 %copy.18 = bf16[128,1728]{0,1:T(8,128)(2,1)} copy(bf16[128,1728]{0,1:T(8,128)(2,1)} %bitcast.18) | data formatting | bytes 884736
  173.5 0.0 slice-start
  173.5 3.3 %copy.19 = bf16[1728,640]{1,0:T(8,128)(2,1)} copy(bf16[1728,640]{1,0:T(8,128)(2,1)} %get-tuple-element.17) | data formatting | bytes 4423680
  176.8 0.0 copy-done.1
  176.8 0.0 slice-start.1
  176.8 2.1 %copy.20 = bf16[5120,432]{0,1:T(8,128)(2,1)} copy(bf16[5120,432]{0,1:T(8,128)(2,1)S(1)} %bitcast.16) | data formatting | bytes 8847360
  178.9 0.0 slice-done
  178.9 0.0 slice-done.1
  178.9 2.1 %copy.21 = bf16[432,5120]{1,0:T(8,128)(2,1)} copy(bf16[432,5120]{1,0:T(8,128)(2,1)S(1)} %bitcast.15) | data formatting | bytes 8847360
  (4 shorter events, 0.0 us)
Async XLA Ops:
  0.6 0.8 copy-start
  171.5 5.3 %copy-start.1 = (bf16[432,5120]{1,0:T(8,128)(2,1)S(1)}, bf16[432,5120]{1,0:T(8,128)(2,1)}, u32[]{:S(2)}) copy-start(bf16[432,5120]{1,0:T(8,128)(2,1)} %get-tuple-element.10) | copy-start | bytes 13271044
  173.5 5.4 %slice-start = ((s8[4423680]{0:T(1024)(128)(4,1)}), s8[4194304]{0:T(1024)(128)(4,1)S(1)}, s32[]{:S(2)}) async-start(s8[4423680]{0:T(1024)(128)(4,1)} %bitcast.14), calls=%async_computation | async-start | bytes 8388608
  176.8 2.1 %slice-start.1 = ((s8[4423680]{0:T(1024)(128)(4,1)}), s8[229376]{0:T(1024)(128)(4,1)S(1)}, s32[]{:S(2)}) async-start(s8[4423680]{0:T(1024)(128)(4,1)} %bitcast.14), calls=%async_computation.1 | async-start | bytes 458752

commit v3 on v2

v3 whole, which is shorter than its diff:
```python
import jax
import jax.numpy as jnp
from jax import lax
from jax.experimental import pallas as pl
from jax.experimental.pallas import tpu as pltpu
from jax.sharding import PartitionSpec as P

MESH = pl.DeviceIdType.MESH
F32 = jnp.float32
BF16 = jnp.bfloat16
GROUPS = 8
ZC = 8


def place():
    g = lax.axis_index("group")
    t = lax.axis_index("tensor")
    return g // 4, g % 4, t // 8, (t // 2) % 4, t % 2


def gid(xl, y):
    return xl * 4 + lax.rem(y, 4)


def tid(xh, z, c):
    return xh * 8 + lax.rem(z, 4) * 2 + c


class Copies:
    def __init__(self, send, recv):
        self.send, self.recv, self.made = send, recv, {}

    def start(self, k, src, dst, dev):
        cp = pltpu.make_async_remote_copy(
            src_ref=src, dst_ref=dst, send_sem=self.send.at[k], recv_sem=self.recv.at[k],
            device_id=dev, device_id_type=MESH,
        )
        cp.start()
        self.made[k] = cp

    def arrived(self, *ks):
        for k in ks:
            self.made[k].wait_recv()

    def finish(self):
        for cp in self.made.values():
            cp.wait_send()


def enter(peers):
    barrier = pltpu.get_barrier_semaphore()
    for dev in peers:
        pl.semaphore_signal(barrier, inc=1, device_id=dev, device_id_type=MESH)
    pl.semaphore_wait(barrier, len(peers))


OWN, ABOVE, BELOW, FAR = 0, 2, 4, 6


class PieceGather:
    def __init__(self, buf, cps, up, down, sib, at):
        self.buf, self.cps, self.up, self.down, self.sib, self.at = buf, cps, up, down, sib, at

    def begin(self, k):
        buf, at, n = self.buf, self.at[k], len(self.at)
        self.cps.start(k, buf.at[(OWN,) + at], buf.at[(BELOW,) + at], self.up)
        self.cps.start(n + k, buf.at[(OWN,) + at], buf.at[(ABOVE,) + at], self.down)

    def middle(self, k):
        buf, at, n = self.buf, self.at[k], len(self.at)
        self.cps.arrived(k, n + k)
        if k % 2 == 0:
            self.cps.start(2 * n + k, buf.at[(BELOW,) + at], buf.at[(FAR,) + at], self.up)
        else:
            self.cps.start(2 * n + k, buf.at[(ABOVE,) + at], buf.at[(FAR,) + at], self.down)

    def share(self, slot):
        self.cps.start(3 * len(self.at) + slot // 2, self.buf.at[slot], self.buf.at[slot + 1], self.sib)

    def shared(self, *slots):
        self.cps.arrived(*(3 * len(self.at) + slot // 2 for slot in slots))

    def last(self):
        n = len(self.at)
        self.cps.arrived(*range(2 * n, 3 * n))
        self.share(FAR)


NT = (((1,), (1,)), ((), ()))
TN = (((0,), (0,)), ((), ()))


def kernel(
    hidden_t, down_h, resid, grad, gain, w_up_t, w_down, sel, sel_back,
    gh_out, gb_out, gu_out, gd_out,
    hid, down, wu, wd, rows, cots, normed,
    acc, sib_out, sib_in, z_out, z_in, x_out, x_in, pick_r, pick_c, resid_v, grad_v,
    pre, dact, act, dpre, act_t, dpre_t, v_out, v_in,
    stage, dn, sd_out, sd_in, far_out, far_in, dir_out, dir_in, sum_out, sum_in,
    drow, back_in, x2_out, x2_in, ds, fp, fin, gh_v,
    a_s, a_r, ca_s, ca_r, cg_s, cg_r, sb_s, sb_r, z_s, z_r, x_s, x_r, ra_s, ra_r, rg_s, rg_r,
    sd_s, sd_r, fr_s, fr_r, nd_s, nd_r, ns_s, ns_r, ba_s, ba_r, x2_s, x2_r, dg_s, dg_r, f_s, f_r, v_s, v_r, local_sem,
):
    where = place()
    xl, y, xh, z, c = where
    g, t = gid(xl, y), tid(xh, z, c)
    me = z * 2 + c
    head = g // 2
    width = resid.shape[1]
    model = rows.shape[2]
    inner = hid.shape[1]
    slots = rows.shape[1]
    part = inner // 2
    quarter = inner // 4

    loads = [pltpu.make_async_copy(hidden_t, hid.at[g], local_sem.at[0])]
    for i in range(2):
        tok = pl.ds(pl.multiple_of((8 * i + me) * 64, 64), 64)
        loads.append(pltpu.make_async_copy(grad.at[tok], grad_v.at[pl.ds(64 * i, 64)], local_sem.at[1 + i]))
        loads.append(pltpu.make_async_copy(resid.at[tok], resid_v.at[pl.ds(64 * i, 64)], local_sem.at[3 + i]))
    late = [
        pltpu.make_async_copy(down_h, down, local_sem.at[5]),
        pltpu.make_async_copy(w_down, wd, local_sem.at[6]),
        pltpu.make_async_copy(w_up_t, wu, local_sem.at[7]),
    ]
    for cp in loads + late[:1]:
        cp.start()

    xp = (gid(1 - xl, y), t)
    yp, ym = (gid(xl, y + 1), t), (gid(xl, y + 3), t)
    sib = (g, tid(xh, z, 1 - c))
    xhp = (g, tid(1 - xh, z, c))
    zup, zdown = (g, tid(xh, z + 1, c)), (g, tid(xh, z + 3, c))
    group_peers = [(lax.rem(g + k, GROUPS), t) for k in range(1, GROUPS)]
    z_peers = [(g, tid(xh, z + k, c)) for k in range(1, 4)]
    cross_peers = [(g, tid(xh, z + k, 1 - c)) for k in range(1, 4)]
    with jax.named_scope("enter"):
        enter(group_peers + z_peers + cross_peers + [sib, xhp])
        for cp in loads:
            cp.wait()

    a, ca, cg, sb = Copies(a_s, a_r), Copies(ca_s, ca_r), Copies(cg_s, cg_r), Copies(sb_s, sb_r)
    xx, ra, rg = Copies(x_s, x_r), Copies(ra_s, ra_r), Copies(rg_s, rg_r)
    sd, fr, nd, ns = Copies(sd_s, sd_r), Copies(fr_s, fr_r), Copies(nd_s, nd_r), Copies(ns_s, ns_r)
    ba, x2, dg, f = Copies(ba_s, ba_r), Copies(x2_s, x2_r), Copies(dg_s, dg_r), Copies(f_s, f_r)
    vx = Copies(v_s, v_r)

    low, high = pl.ds(0, part), pl.ds(part, part)

    def pass_hidden(k, shard, rows_of, to):
        piece = hid.at[shard, rows_of]
        a.start(k, piece, piece, to)

    def cols(j):
        return pl.ds(pl.multiple_of(j * width, 128), width)

    def deal(copies, picked, buf, values):
        picked[...] = jnp.dot(sel[...], values, preferred_element_type=F32).astype(BF16).reshape(picked.shape)
        for k in range(1, GROUPS):
            to = lax.rem(g + k, GROUPS)
            copies.start(k - 1, picked.at[to // 2], buf.at[OWN, :, cols(g)], (to, t))
        buf[OWN, :, cols(g)] = picked[head]

    deal(ca, pick_c, cots, grad_v[...])

    for k, rows_of, to in ((0, low, xp), (2, low, yp), (5, high, ym), (1, high, xp), (3, high, yp), (4, low, ym)):
        pass_hidden(k, g, rows_of, to)
    for cp in late[1:]:
        cp.start()

    columns = [(slice(None), cols(lax.rem(g + GROUPS - k, GROUPS))) for k in range(GROUPS)]
    cot_ring = PieceGather(cots, cg, zup, zdown, sib, columns)
    row_ring = PieceGather(rows, rg, zup, zdown, sib, columns)
    ds_ring = PieceGather(ds, dg, zup, zdown, sib, [(pl.ds(0, 64),), (pl.ds(64, 64),)])

    order = [
        (xl, y), (1 - xl, y), (xl, lax.rem(y + 3, 4)), (xl, lax.rem(y + 1, 4)), (xl, lax.rem(y + 2, 4)),
        (1 - xl, lax.rem(y + 3, 4)), (1 - xl, lax.rem(y + 1, 4)), (1 - xl, lax.rem(y + 2, 4)),
    ]

    def multiply(k):
        sx, sy = order[k]
        acc[k] = lax.dot_general(hid[gid(sx, sy)], down[...], TN, preferred_element_type=F32).reshape(2, 64, width)
        sib_out[k] = acc[k, 1 - c].astype(BF16)
        sb.start(k, sib_out.at[k], sib_in.at[k], sib)

    def z_copy(k):
        sx, sy = order[k]
        return pltpu.make_async_remote_copy(
            src_ref=z_out.at[k], dst_ref=z_in.at[sx, z], send_sem=z_s.at[k], recv_sem=z_r.at[sx, z],
            device_id=(g, tid(xh, sy, c)), device_id_type=MESH,
        )

    def pass_on(k):
        sx, sy = order[k]
        sb.arrived(k)
        z_out[k] = (acc[k, c] + sib_in[k].astype(F32)).astype(BF16)

        @pl.when(sy != z)
        def _():
            z_copy(k).start()

        @pl.when(sy == z)
        def _():
            z_in[sx, z] = z_out[k]

    k_step = 1024

    def product(total, values, weights, lo, hi):
        r = pl.ds(lo * slots, (hi - lo) * slots)
        total[r, :] = jnp.zeros(((hi - lo) * slots, total.shape[1]), F32)

        @pl.loop(0, model // k_step)
        def _(k):
            kc = pl.ds(pl.multiple_of(k * k_step, 128), k_step)
            total[r, :] += lax.dot_general(
                values[lo:hi, :, kc].reshape((hi - lo) * slots, k_step), weights[:, kc], NT,
                preferred_element_type=F32,
            )

    with jax.named_scope("gather_hidden"):
        late[0].wait()
        multiply(0)
        before, after, beside, far = gid(xl, y + 3), gid(xl, y + 1), gid(1 - xl, y), gid(xl, y + 2)
        cot_ring.begin(0)
        for k in range(1, GROUPS):
            ca.arrived(k - 1)
            cot_ring.begin(k)
        cot_ring.share(OWN)
        a.arrived(2)
        pass_hidden(6, before, low, yp)
        a.arrived(5)
        pass_hidden(7, after, high, ym)
        a.arrived(0)
        pass_hidden(8, beside, low, yp)
        pass_hidden(10, beside, low, ym)
        a.arrived(1)
        pass_hidden(9, beside, high, yp)
        pass_hidden(11, beside, high, ym)
        multiply(1)
        pass_on(0)
        a.arrived(3)
        multiply(2)
        pass_on(1)
        a.arrived(4)
        multiply(3)
        pass_on(2)
        a.arrived(6)
        pass_hidden(12, far, low, xp)
        a.arrived(7)
        pass_hidden(13, far, high, xp)
        multiply(4)
        pass_on(3)
        pass_on(4)
    with jax.named_scope("gather_cots"):
        for k in range(GROUPS):
            cot_ring.middle(k)
        cot_ring.share(BELOW)
        cot_ring.share(ABOVE)
    with jax.named_scope("gather_rest"):
        a.arrived(8, 9)
        multiply(5)
        a.arrived(10, 11)
        multiply(6)
        pass_on(5)
        pass_on(6)
        a.arrived(12, 13)
        multiply(7)
        pass_on(7)
    with jax.named_scope("sum_stream"):
        for i, sx in enumerate((xl, 1 - xl)):
            for dz in range(1, 4):
                src = lax.rem(z + dz, 4)
                pltpu.make_async_remote_copy(
                    src_ref=z_out.at[0], dst_ref=z_in.at[sx, src], send_sem=z_s.at[0], recv_sem=z_r.at[sx, src],
                    device_id=(g, tid(xh, z + dz, c)), device_id_type=MESH,
                ).wait_recv()
            parts = z_in[sx].astype(F32)
            x_out[sx] = ((parts[0] + parts[1]) + (parts[2] + parts[3])).astype(BF16)
            xx.start(i, x_out.at[sx], x_in.at[sx], xhp)
        xx.arrived(0, 1)
        total = (x_out[...].astype(F32) + x_in[...].astype(F32)).reshape(2 * 64, width)
        stream = (resid_v[...].astype(F32) + total).astype(BF16)
    with jax.named_scope("deal_rows"):
        deal(ra, pick_r, rows, stream)
        row_ring.begin(0)
        cot_ring.last()
        for k in range(1, GROUPS):
            ra.arrived(k - 1)
            row_ring.begin(k)
        row_ring.share(OWN)

    def gain_at(j):
        return gain[pl.ds(head, 1), cols(j)]

    def norm_shard(slot):
        def add(j, squares):
            v = rows[slot, :, cols(j)].astype(F32)
            return squares + v * v

        squares = lax.fori_loop(0, GROUPS, add, jnp.zeros((slots, width), F32))
        inv = lax.rsqrt(jnp.sum(squares, axis=-1, keepdims=True) * (1.0 / model) + 1e-06)

        @pl.loop(0, GROUPS)
        def _(j):
            v = rows[slot, :, cols(j)].astype(F32)
            normed[slot, :, cols(j)] = (v * inv * gain_at(j)).astype(BF16)

        return inv

    def activate(slot):
        r = pl.ds(slot * slots, slots)
        p = pre[r, :]
        s = jax.nn.sigmoid(p)
        act[r, :] = (p * s).astype(BF16)
        d = (dact[r, :] * s * (1.0 + p * (1.0 - s))).astype(BF16)
        dpre[r, :] = d
        v_out[slot] = jnp.broadcast_to(jnp.sum(d.astype(F32) * p, axis=-1, keepdims=True), v_out.shape[1:])

    with jax.named_scope("gather_rows"):
        cot_ring.shared(OWN, BELOW, ABOVE, FAR)
        late[1].wait()
        late[2].wait()
        inv_own = norm_shard(OWN)
        for k in range(GROUPS):
            row_ring.middle(k)
        row_ring.share(BELOW)
        row_ring.share(ABOVE)
        product(dact, cots, wd, 0, 8)
        row_ring.shared(OWN)
        norm_shard(OWN + 1)
        norm_shard(BELOW)
        norm_shard(ABOVE)
        row_ring.shared(BELOW)
        row_ring.shared(ABOVE)
        norm_shard(BELOW + 1)
        norm_shard(ABOVE + 1)
        row_ring.last()
        product(pre, normed, wu, 0, FAR)
        for slot in range(FAR):
            activate(slot)
        norm_shard(FAR)
        row_ring.shared(FAR)
        norm_shard(FAR + 1)

    with jax.named_scope("heads"):
        product(pre, normed, wu, FAR, 8)
        activate(FAR)
        activate(FAR + 1)
        for slot in range(1, 8):
            core = 1 - c if slot % 2 else c
            vx.start(slot - 1, v_out.at[slot], v_in.at[slot], (g, tid(xh, z + (0, 1, 3, 2)[slot // 2], core)))

    def dn_multiply(i):
        stage[...] = jnp.dot(
            dpre[...], wu[:, cols(lax.rem(g + i, GROUPS))], preferred_element_type=F32
        ).reshape(stage.shape)
        dn[i] = stage[:, 0]
        sd_out[i] = stage[:, 1].astype(BF16)
        sd.start(i, sd_out.at[i], sd_in.at[i], sib)

    def toward(i):
        return (zup, zdown, ABOVE // 2, BELOW // 2) if i % 2 == 0 else (zdown, zup, BELOW // 2, ABOVE // 2)

    def dn_split(i):
        to, other, z_to, z_other = toward(i)
        sd.arrived(i)
        dn[i] = dn[i] + sd_in[i].astype(F32)
        far_out[i] = dn[i, FAR // 2].astype(BF16)
        fr.start(i, far_out.at[i], far_in.at[i], to)
        dir_out[i] = dn[i, z_other].astype(BF16)
        nd.start(i, dir_out.at[i], dir_in.at[i], other)

    def dn_forward(i):
        to, other, z_to, z_other = toward(i)
        fr.arrived(i)
        sum_out[i] = (dn[i, z_to] + far_in[i].astype(F32)).astype(BF16)
        ns.start(i, sum_out.at[i], sum_in.at[i], to)

    def dn_finish(i):
        to = lax.rem(g + i, GROUPS)
        ns.arrived(i)
        nd.arrived(i)
        q = (dn[i, 0] + sum_in[i].astype(F32) + dir_in[i].astype(F32)) * gain_at(to)
        value = (inv_own * q - rows[OWN, :, cols(to)].astype(F32) * back).astype(BF16)
        if i == 0:
            back_in[g] = value
        else:
            drow[i] = value
            ba.start(i - 1, drow.at[i], back_in.at[g], (to, t))

    with jax.named_scope("row_gradients"):
        for i in range(GROUPS + 3):
            if i < 8:
                dn_multiply(i)
            if 0 <= i - 1 < 8:
                dn_split(i - 1)
            if 0 <= i - 3 < 8:
                dn_forward(i - 3)
        vx.arrived(*range(7))
        v = v_out[0]
        for slot in range(1, 8):
            v = v + v_in[slot]
        back = inv_own * inv_own * (v[:, :1] * (1.0 / model))

    def down_grad(j):
        wd[:, cols(j)] = jnp.dot(
            act_t[...], cots[:, :, cols(j)].reshape(ZC * slots, width), preferred_element_type=F32
        ).astype(BF16)

    def up_grad(j):
        wu[:, cols(j)] = jnp.dot(
            dpre_t[...], normed[:, :, cols(j)].reshape(ZC * slots, width), preferred_element_type=F32
        ).astype(BF16)

    with jax.named_scope("down_grads"):
        act_t[...] = act[...].T
        dpre_t[...] = dpre[...].T
        for i in range(3):
            dn_finish(i)
        pl.loop(0, GROUPS)(down_grad)
        gd_copy = pltpu.make_async_copy(wd, gd_out, local_sem.at[0])
        gd_copy.start()

    with jax.named_scope("norm_backward"):
        for i in range(3, GROUPS):
            dn_finish(i)

    with jax.named_scope("return_rows"):
        pl.loop(0, 3)(up_grad)
        ba.arrived(*range(GROUPS - 1))
        x2_out[...] = jnp.dot(
            sel_back[...], back_in[...].reshape(GROUPS * slots, width), preferred_element_type=F32
        ).astype(BF16)
        halves = (pl.ds(0, 64), pl.ds(64, 64))
        for i, h in enumerate(halves):
            x2.start(i, x2_out.at[h], x2_in.at[h], xhp)
        for i, h in enumerate(halves):
            x2.arrived(i)
            ds[OWN, h, :] = (
                grad_v[h, :].astype(F32) + (x2_out[h, :].astype(F32) + x2_in[h, :].astype(F32))
            ).astype(BF16)
            ds_ring.begin(i)
        ds_ring.share(OWN)
    with jax.named_scope("gather_dstream"):
        pl.loop(3, GROUPS)(up_grad)
        gu_copy = pltpu.make_async_copy(wu, gu_out, local_sem.at[1])
        gu_copy.start()
        ds_ring.middle(0)
        ds_ring.middle(1)
        ds_ring.share(BELOW)
        ds_ring.share(ABOVE)
        ds_ring.last()
        ds_ring.shared(OWN, BELOW, ABOVE, FAR)

    def tokens_of(sx, sy):
        ahead = lax.rem(sy + 4 - z, 4)
        slot = jnp.where(ahead == 3, BELOW, jnp.where(ahead == 2, FAR, ahead * 2))
        at = pl.ds(pl.multiple_of(sx * 64, 64), 64)
        return [ds[slot + c, at, :], ds[slot + 1 - c, at, :]]

    def hidden_grads(i, first, second, r):
        both = jnp.concatenate(tokens_of(*first) + tokens_of(*second), axis=0)
        p = lax.dot_general(down[r, :], both, NT, preferred_element_type=F32).astype(BF16)
        fp[i, r, :] = p[:, :128]
        fp[i + 1, r, :] = p[:, 128:]

    y1, y2, y3 = lax.rem(y + 1, 4), lax.rem(y + 2, 4), lax.rem(y + 3, 4)
    quarters = [pl.ds(m * quarter, quarter) for m in range(4)]

    def f_start(kind, m, src, dst, to):
        r = quarters[m]
        f.start(kind * 4 + m, fp.at[src, r], fin.at[dst, r], to)

    def f_sum(dst, m, *terms):
        r = quarters[m]
        total = fp[dst, r, :].astype(F32)
        for term in terms:
            total = total + fin[term, r, :].astype(F32)
        return total.astype(BF16)

    def f_begin(m):
        r = quarters[m]
        hidden_grads(2, (1 - xl, y1), (1 - xl, y3), r)
        f_start(0, m, 2, 0, yp)
        f_start(1, m, 3, 1, ym)
        hidden_grads(0, (1 - xl, y2), (xl, y2), r)
        f_start(2, m, 0, 2, xp)
        hidden_grads(4, (xl, y1), (xl, y3), r)
        if m % 2 == 0:
            f_start(3, m, 5, 4, ym)
        else:
            f_start(3, m, 4, 3, yp)
        hidden_grads(6, (1 - xl, y), (xl, y), r)

    def f_far(m):
        f.arrived(8 + m)
        fp[1, quarters[m], :] = f_sum(1, m, 2)
        f_start(4, m, 1, 6, yp if m % 2 == 0 else ym)

    def f_side(m):
        f.arrived(m, 4 + m)
        fp[6, quarters[m], :] = f_sum(6, m, 0, 1)
        f_start(5, m, 6, 5, xp)

    def f_near(m):
        f.arrived(16 + m)
        i = 4 if m % 2 == 0 else 5
        fp[i, quarters[m], :] = f_sum(i, m, 6)
        f_start(6, m, i, i - 1, yp if m % 2 == 0 else ym)

    def f_end(m):
        f.arrived(12 + m, 20 + m, 24 + m)
        gh_v[quarters[m], :] = f_sum(7, m, 3, 4, 5)

    def backbone_grad(m):
        r = pl.ds(pl.multiple_of(m * quarter, 16), quarter)
        total = jnp.zeros((quarter, width), F32)
        for i in range(4):
            left = jnp.concatenate([hid[2 * i, r, :], hid[2 * i + 1, r, :]], axis=1)
            right = jnp.concatenate(
                tokens_of((2 * i) // 4, (2 * i) % 4) + tokens_of((2 * i + 1) // 4, (2 * i + 1) % 4), axis=0)
            total = total + jnp.dot(left, right, preferred_element_type=F32)
        down[r, :] = total.astype(BF16)

    with jax.named_scope("hidden_grads"):
        for m in range(4):
            f_begin(m)
    with jax.named_scope("sum_hidden_grads"):
        f_far(0)
        f_far(1)
        f_side(0)
        f_far(2)
        f_far(3)
        pl.loop(0, 2)(backbone_grad)
        f_side(1)
        f_near(0)
        f_near(1)
        f_side(2)
        f_side(3)
        pl.loop(2, 4)(backbone_grad)
        gb_copy = pltpu.make_async_copy(down, gb_out, local_sem.at[2])
        gb_copy.start()
        f_near(2)
        f_near(3)
        for m in range(4):
            f_end(m)
        gh_copy = pltpu.make_async_copy(gh_v, gh_out, local_sem.at[3])
        gh_copy.start()

    with jax.named_scope("finish"):
        for cps in (a, ca, cg, sb, xx, ra, rg, sd, fr, nd, ns, ba, x2, dg, f, vx):
            cps.finish()
        for k in range(GROUPS):
            @pl.when(order[k][1] != z)
            def _():
                z_copy(k).wait_send()
        for cp in (gd_copy, gu_copy, gb_copy, gh_copy):
            cp.wait()


def run(hidden_t, down, resid, grad, gain, w_up_t, w_down, sel, sel_back):
    inner, tokens = hidden_t.shape
    width = down.shape[1]
    slots = sel.shape[0] // 4
    model = width * GROUPS
    units = w_down.shape[0]
    any_spec = pl.BlockSpec(memory_space=pl.ANY)
    vmem = pl.BlockSpec(memory_space=pltpu.VMEM)
    dma = pltpu.SemaphoreType.DMA
    sems = []
    for n in ((14,), (7,), (28,), (8,)):
        sems += [dma(n), dma(n)]
    sems += [dma((8,)), dma((2, 4))]
    for n in ((2,), (7,), (28,), (8,), (8,), (8,), (8,), (7,), (2,), (10,), (28,), (7,)):
        sems += [dma(n), dma(n)]
    sems += [dma((8,))]
    piece = (64, width)
    return pl.pallas_call(
        kernel,
        out_shape=(
            jax.ShapeDtypeStruct((inner, tokens), BF16),
            jax.ShapeDtypeStruct((inner, width), BF16),
            jax.ShapeDtypeStruct((units, model), BF16),
            jax.ShapeDtypeStruct((units, model), BF16),
        ),
        in_specs=[any_spec] * 4 + [vmem] + [any_spec] * 2 + [vmem] * 2,
        out_specs=(any_spec,) * 4,
        scratch_shapes=[
            pltpu.VMEM((GROUPS, inner, tokens), BF16),
            pltpu.VMEM((inner, width), BF16),
            pltpu.VMEM((units, model), BF16),
            pltpu.VMEM((units, model), BF16),
            pltpu.VMEM((ZC, slots, model), BF16),
            pltpu.VMEM((ZC, slots, model), BF16),
            pltpu.VMEM((ZC, slots, model), BF16),
            pltpu.VMEM((8, 2) + piece, F32),
            pltpu.VMEM((8,) + piece, BF16),
            pltpu.VMEM((8,) + piece, BF16),
            pltpu.VMEM((8,) + piece, BF16),
            pltpu.VMEM((2, 4) + piece, BF16),
            pltpu.VMEM((2,) + piece, BF16),
            pltpu.VMEM((2,) + piece, BF16),
            pltpu.VMEM((4, slots, width), BF16),
            pltpu.VMEM((4, slots, width), BF16),
            pltpu.VMEM((128, width), BF16),
            pltpu.VMEM((128, width), BF16),
            pltpu.VMEM((ZC * slots, units), F32),
            pltpu.VMEM((ZC * slots, units), F32),
            pltpu.VMEM((ZC * slots, units), BF16),
            pltpu.VMEM((ZC * slots, units), BF16),
            pltpu.VMEM((units, ZC * slots), BF16),
            pltpu.VMEM((units, ZC * slots), BF16),
            pltpu.VMEM((ZC, slots, 128), F32),
            pltpu.VMEM((ZC, slots, 128), F32),
            pltpu.VMEM((4, 2, slots, width), F32),
            pltpu.VMEM((8, 4, slots, width), F32),
            pltpu.VMEM((8, 4, slots, width), BF16),
            pltpu.VMEM((8, 4, slots, width), BF16),
        ]
        + [pltpu.VMEM((8, slots, width), BF16)] * 6
        + [
            pltpu.VMEM((8, slots, width), BF16),
            pltpu.VMEM((8, slots, width), BF16),
            pltpu.VMEM((128, width), BF16),
            pltpu.VMEM((128, width), BF16),
            pltpu.VMEM((8, 128, width), BF16),
            pltpu.VMEM((8, inner, tokens), BF16),
            pltpu.VMEM((7, inner, tokens), BF16),
            pltpu.VMEM((inner, tokens), BF16),
        ]
        + sems,
        compiler_params=pltpu.CompilerParams(
            collective_id=0, has_side_effects=True, vmem_limit_bytes=62 * 1024 * 1024
        ),
        name="backbone_and_heads",
    )(hidden_t, down, resid, grad, gain, w_up_t, w_down, sel, sel_back)


def copy_kernel(*refs):
    n = (len(refs) - 2) // 3
    held, sem_in, sem_out = refs[2 * n : 3 * n], refs[-2], refs[-1]
    copies = []
    for src, mid, dst in zip(refs[:n], held, refs[n : 2 * n]):
        step = src.shape[0] // 3
        for r in range(0, src.shape[0], step):
            rows_of, k = pl.ds(r, step), len(copies)
            copies.append((
                pltpu.make_async_copy(src.at[rows_of], mid.at[rows_of], sem_in.at[k]),
                pltpu.make_async_copy(mid.at[rows_of], dst.at[rows_of], sem_out.at[k]),
            ))
    for fetch, _ in copies:
        fetch.start()
    for fetch, store in copies:
        fetch.wait()
        store.start()
    for _, store in copies:
        store.wait()


def place_results(*arrays):
    any_spec = pl.BlockSpec(memory_space=pl.ANY)
    count = 3 * len(arrays)
    return pl.pallas_call(
        copy_kernel,
        out_shape=tuple(jax.ShapeDtypeStruct(a.shape, a.dtype) for a in arrays),
        in_specs=[any_spec] * len(arrays),
        out_specs=(any_spec,) * len(arrays),
        scratch_shapes=[pltpu.VMEM(a.shape, a.dtype) for a in arrays]
        + [pltpu.SemaphoreType.DMA((count,)), pltpu.SemaphoreType.DMA((count,))],
        compiler_params=pltpu.CompilerParams(vmem_limit_bytes=62 * 1024 * 1024),
        name="place_results",
    )(*arrays)


def local(backbone_hidden, backbone_down, residual, head_grad, gain, w_up, w_down, route):
    groups = lax.axis_size("group")
    heads = gain.shape[0]
    zc = lax.rem(lax.axis_index("tensor"), ZC)
    blocks, _, slot_count = route.shape
    block_len = residual.shape[0] // blocks
    own = lax.dynamic_index_in_dim(route.reshape(2, ZC, heads, slot_count), zc, 1, keepdims=False)
    wanted = jnp.where(own >= 0, own + (jnp.arange(2, dtype=jnp.int32) * block_len)[:, None, None], -1)
    wanted = wanted.transpose(1, 0, 2).reshape(heads, 2 * slot_count)
    positions = jnp.arange(2 * block_len, dtype=jnp.int32)
    sel = (wanted.reshape(-1)[:, None] == positions[None]).astype(BF16)
    twice = jnp.repeat(wanted, groups // heads, axis=0).reshape(-1)
    sel_back = (positions[:, None] == twice[None]).astype(BF16)
    gh, gb, gu, gd = run(
        backbone_hidden.T, backbone_down, residual, head_grad, gain, w_up.T, w_down, sel, sel_back
    )
    gh, gb, gu, gd = place_results(gh, gb, gu, gd)
    return (gh.T, gb, gu.T, gd)


def solution(mesh):
    placed = (
        P("group", "tensor"),
        P("tensor", "group"),
        P(None, "group"),
        P(None, "group"),
        P(),
        P(None, ("group", "tensor")),
        P(("group", "tensor"), None),
        P(),
    )
    return jax.shard_map(
        local,
        mesh=mesh,
        in_specs=placed,
        out_specs=(
            P("group", "tensor"),
            P("tensor", "group"),
            P(None, ("group", "tensor")),
            P(("group", "tensor"), None),
        ),
        check_vma=False,
    )
```

time: 181 us -> 169 us (0.934)
  local copies, waits for them, and re-layouts: 10.5 us -> 1 us
  Pallas kernels: 168 us -> 166 us
    pallas_call x1, Pallas kernels: 168 us -> 157 us  [run(): pl.pallas_call(kernel, out_shape=(jax.ShapeDtypeStruct((inner, tokens), B...]
    unnamed x12 -> x2, local copies, waits for them, and re-layouts: 10.2 us -> 0.75 us
    pallas_call x0 -> x1, Pallas kernels: none -> 8.79 us  [place_results(): pl.pallas_call(copy_kernel, out_shape=tuple((jax.ShapeDtypeStruct(a.shape...]
where the time goes in v3:
time: 169 us
  Pallas kernels  166 us (98%)
    pallas_call x1, Pallas kernels, run(): pl.pallas_call(kernel, out_shape=(jax.ShapeDtypeStruct((inner, tokens), B...  157 us
    pallas_call x1, Pallas kernels, place_results(): pl.pallas_call(copy_kernel, out_shape=tuple((jax.ShapeDtypeStruct(a.shape...  8.79 us

profile of v3, /device:TPU:1, one launch (start us, length us, event | category | flops | bytes accessed | tf_op | source)
XLA Modules:
  0.0 168.9 jit_solution(12822706020271653212)
XLA Ops:
  0.6 0.0 copy-start
  0.7 0.7 copy-done
  1.4 0.1 fusion.2
  1.5 0.1 eq.30
  1.6 0.1 reshape.21
  1.6 0.1 eq.35
  1.7 0.7 fusion.1.sel
  2.5 0.7 fusion.sel_back
  3.1 156.8 %backbone_and_heads.1 = (bf16[1728,128]{1,0:T(8,128)(2,1)}, bf16[1728,640]{1,0:T(8,128)(2,1)}, bf16[432,5120]{1,0:T(8,128)(2,1)}, bf16[432,5120]{1,0:T(8,128)(2,1)}) custom-call(bf16[1728,128]{1,0:T(8,128)(2,1)} %bitcast.14, bf16[1728,640]{1,0:T(8,128)(2,1)} %down_h.1, bf16[1024,640]{1,0:T(8,128)(2,1)} %resid.1, bf16[1024,640]{1,0:T(8,128)(2,1)} %grad.1, ...), custom_call_target="tpu_custom_call" | custom-call | tf_op jit(solution)/shard_map/backbone_and_heads/pallas_call | solution.py:579
  159.9 8.8 %place_results.1 = (bf16[1728,128]{1,0:T(8,128)(2,1)}, bf16[1728,640]{1,0:T(8,128)(2,1)}, bf16[432,5120]{1,0:T(8,128)(2,1)}, bf16[432,5120]{1,0:T(8,128)(2,1)}) custom-call(bf16[1728,128]{1,0:T(8,128)(2,1)} %get-tuple-element.12.refs_0_, bf16[1728,640]{1,0:T(8,128)(2,1)} %get-tuple-element.13.refs_1_, bf16[432,5120]{1,0:T(8,128)(2,1)} %get-tuple-element.14.refs_2_, ...), custom_call_target="tpu_custom_call" | custom-call | tf_op jit(solution)/shard_map/place_results/pallas_call | solution.py:664
  (3 shorter events, 0.0 us)
Async XLA Ops:
  0.6 0.8 copy-start

commit v4 on v3

--- a/solution.py
+++ b/solution.py
@@ -91,13 +91,13 @@
 
 
 def kernel(
-    hidden_t, down_h, resid, grad, gain, w_up_t, w_down, sel, sel_back,
-    gh_out, gb_out, gu_out, gd_out,
-    hid, down, wu, wd, rows, cots, normed,
+    hidden_t, down_h, resid, grad, gain_h, w_up_t, w_down, places,
+    gh_v, down, wu, wd,
+    hid, gain, sel_of, rows, cots, normed,
     acc, sib_out, sib_in, z_out, z_in, x_out, x_in, pick_r, pick_c, resid_v, grad_v,
     pre, dact, act, dpre, act_t, dpre_t, v_out, v_in,
     stage, dn, sd_out, sd_in, far_out, far_in, dir_out, dir_in, sum_out, sum_in,
-    drow, back_in, x2_out, x2_in, ds, fp, fin, gh_v,
+    drow, back_in, x2_out, x2_in, ds, fp, fin,
     a_s, a_r, ca_s, ca_r, cg_s, cg_r, sb_s, sb_r, z_s, z_r, x_s, x_r, ra_s, ra_r, rg_s, rg_r,
     sd_s, sd_r, fr_s, fr_r, nd_s, nd_r, ns_s, ns_r, ba_s, ba_r, x2_s, x2_r, dg_s, dg_r, f_s, f_r, v_s, v_r, local_sem,
 ):
@@ -118,6 +118,8 @@
         tok = pl.ds(pl.multiple_of((8 * i + me) * 64, 64), 64)
         loads.append(pltpu.make_async_copy(grad.at[tok], grad_v.at[pl.ds(64 * i, 64)], local_sem.at[1 + i]))
         loads.append(pltpu.make_async_copy(resid.at[tok], resid_v.at[pl.ds(64 * i, 64)], local_sem.at[3 + i]))
+    loads.append(pltpu.make_async_copy(places, sel_of, local_sem.at[8]))
+    loads.append(pltpu.make_async_copy(gain_h, gain, local_sem.at[9]))
     late = [
         pltpu.make_async_copy(down_h, down, local_sem.at[5]),
         pltpu.make_async_copy(w_down, wd, local_sem.at[6]),
@@ -154,8 +156,18 @@
     def cols(j):
         return pl.ds(pl.multiple_of(j * width, 128), width)
 
+    def select():
+        lane = lax.broadcasted_iota(jnp.int32, (128, 4 * slots), 1)
+        token = lax.broadcasted_iota(jnp.int32, (128, 4 * slots), 0)
+        second = lax.rem(lane, slots) >= slots // 2
+        places = [sel_of[8 * i + me, h : h + 1, :] for h in range(4) for i in range(2)]
+        wanted = jnp.broadcast_to(jnp.concatenate(places, axis=1), lane.shape)
+        hit = (wanted >= 0) & (wanted + jnp.where(second, 64, 0) == token)
+        return jnp.where(hit, 1.0, 0.0).astype(BF16)
+
     def deal(copies, picked, buf, values):
-        picked[...] = jnp.dot(sel[...], values, preferred_element_type=F32).astype(BF16).reshape(picked.shape)
+        chosen = lax.dot_general(select(), values, TN, preferred_element_type=F32)
+        picked[...] = chosen.astype(BF16).reshape(picked.shape)
         for k in range(1, GROUPS):
             to = lax.rem(g + k, GROUPS)
             copies.start(k - 1, picked.at[to // 2], buf.at[OWN, :, cols(g)], (to, t))
@@ -322,11 +334,11 @@
         late[1].wait()
         late[2].wait()
         inv_own = norm_shard(OWN)
+        product(dact, cots, wd, 0, 8)
         for k in range(GROUPS):
             row_ring.middle(k)
         row_ring.share(BELOW)
         row_ring.share(ABOVE)
-        product(dact, cots, wd, 0, 8)
         row_ring.shared(OWN)
         norm_shard(OWN + 1)
         norm_shard(BELOW)
@@ -384,10 +396,10 @@
         q = (dn[i, 0] + sum_in[i].astype(F32) + dir_in[i].astype(F32)) * gain_at(to)
         value = (inv_own * q - rows[OWN, :, cols(to)].astype(F32) * back).astype(BF16)
         if i == 0:
-            back_in[g] = value
+            back_in[lax.rem(g, 2), head] = value
         else:
             drow[i] = value
-            ba.start(i - 1, drow.at[i], back_in.at[g], (to, t))
+            ba.start(i - 1, drow.at[i], back_in.at[lax.rem(g, 2), head], (to, t))
 
     with jax.named_scope("row_gradients"):
         for i in range(GROUPS + 3):
@@ -416,25 +428,23 @@
     with jax.named_scope("down_grads"):
         act_t[...] = act[...].T
         dpre_t[...] = dpre[...].T
-        for i in range(3):
+    with jax.named_scope("norm_backward"):
+        for i in range(GROUPS):
             dn_finish(i)
-        pl.loop(0, GROUPS)(down_grad)
-        gd_copy = pltpu.make_async_copy(wd, gd_out, local_sem.at[0])
-        gd_copy.start()
-
-    with jax.named_scope("norm_backward"):
-        for i in range(3, GROUPS):
-            dn_finish(i)
 
     with jax.named_scope("return_rows"):
-        pl.loop(0, 3)(up_grad)
+        pl.loop(0, 4)(down_grad)
         ba.arrived(*range(GROUPS - 1))
-        x2_out[...] = jnp.dot(
-            sel_back[...], back_in[...].reshape(GROUPS * slots, width), preferred_element_type=F32
+        chosen = select()
+        x2_out[...] = (
+            jnp.dot(chosen, back_in[0].reshape(4 * slots, width), preferred_element_type=F32)
+            + jnp.dot(chosen, back_in[1].reshape(4 * slots, width), preferred_element_type=F32)
         ).astype(BF16)
         halves = (pl.ds(0, 64), pl.ds(64, 64))
         for i, h in enumerate(halves):
             x2.start(i, x2_out.at[h], x2_in.at[h], xhp)
+        pl.loop(4, GROUPS)(down_grad)
+        pl.loop(0, 3)(up_grad)
         for i, h in enumerate(halves):
             x2.arrived(i)
             ds[OWN, h, :] = (
@@ -443,9 +453,7 @@
             ds_ring.begin(i)
         ds_ring.share(OWN)
     with jax.named_scope("gather_dstream"):
-        pl.loop(3, GROUPS)(up_grad)
-        gu_copy = pltpu.make_async_copy(wu, gu_out, local_sem.at[1])
-        gu_copy.start()
+        pl.loop(3, 6)(up_grad)
         ds_ring.middle(0)
         ds_ring.middle(1)
         ds_ring.share(BELOW)
@@ -487,16 +495,18 @@
         hidden_grads(0, (1 - xl, y2), (xl, y2), r)
         f_start(2, m, 0, 2, xp)
         hidden_grads(4, (xl, y1), (xl, y3), r)
+        hidden_grads(6, (1 - xl, y), (xl, y), r)
+
+    def f_far(m):
+        f.arrived(8 + m)
+        fp[1, quarters[m], :] = f_sum(1, m, 2)
+        f_start(4, m, 1, 6, yp if m % 2 == 0 else ym)
+
+    def f_direct(m):
         if m % 2 == 0:
             f_start(3, m, 5, 4, ym)
         else:
             f_start(3, m, 4, 3, yp)
-        hidden_grads(6, (1 - xl, y), (xl, y), r)
-
-    def f_far(m):
-        f.arrived(8 + m)
-        fp[1, quarters[m], :] = f_sum(1, m, 2)
-        f_start(4, m, 1, 6, yp if m % 2 == 0 else ym)
 
     def f_side(m):
         f.arrived(m, 4 + m)
@@ -527,11 +537,12 @@
         for m in range(4):
             f_begin(m)
     with jax.named_scope("sum_hidden_grads"):
-        f_far(0)
-        f_far(1)
+        for m in range(4):
+            f_far(m)
+        for m in range(4):
+            f_direct(m)
         f_side(0)
-        f_far(2)
-        f_far(3)
+        pl.loop(6, 8)(up_grad)
         pl.loop(0, 2)(backbone_grad)
         f_side(1)
         f_near(0)
@@ -539,14 +550,10 @@
         f_side(2)
         f_side(3)
         pl.loop(2, 4)(backbone_grad)
-        gb_copy = pltpu.make_async_copy(down, gb_out, local_sem.at[2])
-        gb_copy.start()
         f_near(2)
         f_near(3)
         for m in range(4):
             f_end(m)
-        gh_copy = pltpu.make_async_copy(gh_v, gh_out, local_sem.at[3])
-        gh_copy.start()
 
     with jax.named_scope("finish"):
         for cps in (a, ca, cg, sb, xx, ra, rg, sd, fr, nd, ns, ba, x2, dg, f, vx):
@@ -555,14 +562,12 @@
             @pl.when(order[k][1] != z)
             def _():
                 z_copy(k).wait_send()
-        for cp in (gd_copy, gu_copy, gb_copy, gh_copy):
-            cp.wait()
-
-
-def run(hidden_t, down, resid, grad, gain, w_up_t, w_down, sel, sel_back):
+
+
+def run(hidden_t, down, resid, grad, gain, w_up_t, w_down, places):
     inner, tokens = hidden_t.shape
     width = down.shape[1]
-    slots = sel.shape[0] // 4
+    slots = 2 * places.shape[2]
     model = width * GROUPS
     units = w_down.shape[0]
     any_spec = pl.BlockSpec(memory_space=pl.ANY)
@@ -574,23 +579,22 @@
     sems += [dma((8,)), dma((2, 4))]
     for n in ((2,), (7,), (28,), (8,), (8,), (8,), (8,), (7,), (2,), (10,), (28,), (7,)):
         sems += [dma(n), dma(n)]
-    sems += [dma((8,))]
+    sems += [dma((10,))]
     piece = (64, width)
     return pl.pallas_call(
         kernel,
         out_shape=(
-            jax.ShapeDtypeStruct((inner, tokens), BF16),
-            jax.ShapeDtypeStruct((inner, width), BF16),
-            jax.ShapeDtypeStruct((units, model), BF16),
-            jax.ShapeDtypeStruct((units, model), BF16),
-        ),
-        in_specs=[any_spec] * 4 + [vmem] + [any_spec] * 2 + [vmem] * 2,
-        out_specs=(any_spec,) * 4,
-        scratch_shapes=[
-            pltpu.VMEM((GROUPS, inner, tokens), BF16),
+            pltpu.VMEM((inner, tokens), BF16),
             pltpu.VMEM((inner, width), BF16),
             pltpu.VMEM((units, model), BF16),
             pltpu.VMEM((units, model), BF16),
+        ),
+        in_specs=[any_spec] * 8,
+        out_specs=(vmem,) * 4,
+        scratch_shapes=[
+            pltpu.VMEM((GROUPS, inner, tokens), BF16),
+            pltpu.VMEM((4, model), F32),
+            pltpu.VMEM(places.shape, jnp.int32),
             pltpu.VMEM((ZC, slots, model), BF16),
             pltpu.VMEM((ZC, slots, model), BF16),
             pltpu.VMEM((ZC, slots, model), BF16),
@@ -621,73 +625,50 @@
         + [pltpu.VMEM((8, slots, width), BF16)] * 6
         + [
             pltpu.VMEM((8, slots, width), BF16),
-            pltpu.VMEM((8, slots, width), BF16),
+            pltpu.VMEM((2, 4, slots, width), BF16),
             pltpu.VMEM((128, width), BF16),
             pltpu.VMEM((128, width), BF16),
             pltpu.VMEM((8, 128, width), BF16),
             pltpu.VMEM((8, inner, tokens), BF16),
             pltpu.VMEM((7, inner, tokens), BF16),
-            pltpu.VMEM((inner, tokens), BF16),
         ]
         + sems,
         compiler_params=pltpu.CompilerParams(
-            collective_id=0, has_side_effects=True, vmem_limit_bytes=62 * 1024 * 1024
+            collective_id=0, has_side_effects=True, vmem_limit_bytes=50 * 1024 * 1024
         ),
         name="backbone_and_heads",
-    )(hidden_t, down, resid, grad, gain, w_up_t, w_down, sel, sel_back)
+    )(hidden_t, down, resid, grad, gain, w_up_t, w_down, places)
 
 
 def copy_kernel(*refs):
-    n = (len(refs) - 2) // 3
-    held, sem_in, sem_out = refs[2 * n : 3 * n], refs[-2], refs[-1]
+    n = (len(refs) - 1) // 2
     copies = []
-    for src, mid, dst in zip(refs[:n], held, refs[n : 2 * n]):
+    for src, dst in zip(refs[:n], refs[n : 2 * n]):
         step = src.shape[0] // 3
         for r in range(0, src.shape[0], step):
-            rows_of, k = pl.ds(r, step), len(copies)
-            copies.append((
-                pltpu.make_async_copy(src.at[rows_of], mid.at[rows_of], sem_in.at[k]),
-                pltpu.make_async_copy(mid.at[rows_of], dst.at[rows_of], sem_out.at[k]),
-            ))
-    for fetch, _ in copies:
-        fetch.start()
-    for fetch, store in copies:
-        fetch.wait()
-        store.start()
-    for _, store in copies:
-        store.wait()
+            rows_of = pl.ds(r, step)
+            copies.append(pltpu.make_async_copy(src.at[rows_of], dst.at[rows_of], refs[-1].at[len(copies)]))
+    for cp in copies:
+        cp.start()
+    for cp in copies:
+        cp.wait()
 
 
 def place_results(*arrays):
-    any_spec = pl.BlockSpec(memory_space=pl.ANY)
-    count = 3 * len(arrays)
     return pl.pallas_call(
         copy_kernel,
         out_shape=tuple(jax.ShapeDtypeStruct(a.shape, a.dtype) for a in arrays),
-        in_specs=[any_spec] * len(arrays),
-        out_specs=(any_spec,) * len(arrays),
-        scratch_shapes=[pltpu.VMEM(a.shape, a.dtype) for a in arrays]
-        + [pltpu.SemaphoreType.DMA((count,)), pltpu.SemaphoreType.DMA((count,))],
-        compiler_params=pltpu.CompilerParams(vmem_limit_bytes=62 * 1024 * 1024),
+        in_specs=[pl.BlockSpec(memory_space=pltpu.VMEM)] * len(arrays),
+        out_specs=(pl.BlockSpec(memory_space=pl.ANY),) * len(arrays),
+        scratch_shapes=[pltpu.SemaphoreType.DMA((3 * len(arrays),))],
+        compiler_params=pltpu.CompilerParams(vmem_limit_bytes=4 * 1024 * 1024),
         name="place_results",
     )(*arrays)
 
 
 def local(backbone_hidden, backbone_down, residual, head_grad, gain, w_up, w_down, route):
-    groups = lax.axis_size("group")
-    heads = gain.shape[0]
-    zc = lax.rem(lax.axis_index("tensor"), ZC)
-    blocks, _, slot_count = route.shape
-    block_len = residual.shape[0] // blocks
-    own = lax.dynamic_index_in_dim(route.reshape(2, ZC, heads, slot_count), zc, 1, keepdims=False)
-    wanted = jnp.where(own >= 0, own + (jnp.arange(2, dtype=jnp.int32) * block_len)[:, None, None], -1)
-    wanted = wanted.transpose(1, 0, 2).reshape(heads, 2 * slot_count)
-    positions = jnp.arange(2 * block_len, dtype=jnp.int32)
-    sel = (wanted.reshape(-1)[:, None] == positions[None]).astype(BF16)
-    twice = jnp.repeat(wanted, groups // heads, axis=0).reshape(-1)
-    sel_back = (positions[:, None] == twice[None]).astype(BF16)
     gh, gb, gu, gd = run(
-        backbone_hidden.T, backbone_down, residual, head_grad, gain, w_up.T, w_down, sel, sel_back
+        backbone_hidden.T, backbone_down, residual, head_grad, gain, w_up.T, w_down, route
     )
     gh, gb, gu, gd = place_results(gh, gb, gu, gd)
     return (gh.T, gb, gu.T, gd)

time: 169 us -> 155 us (0.917)
  Pallas kernels: 166 us -> 154 us
    pallas_call x1, Pallas kernels: 157 us -> 150 us  [run(): pl.pallas_call(kernel, out_shape=(pltpu.VMEM((inner, tokens), BF16), pltp...]
    pallas_call x1, Pallas kernels: 8.79 us -> 4.39 us  [place_results(): pl.pallas_call(copy_kernel, out_shape=tuple((jax.ShapeDtypeStruct(a.shape...]
where the time goes in v4:
time: 155 us
  Pallas kernels  154 us (99%)
    pallas_call x1, Pallas kernels, run(): pl.pallas_call(kernel, out_shape=(pltpu.VMEM((inner, tokens), BF16), pltp...  150 us
    pallas_call x1, Pallas kernels, place_results(): pl.pallas_call(copy_kernel, out_shape=tuple((jax.ShapeDtypeStruct(a.shape...  4.39 us

profile of v4, /device:TPU:1, one launch (start us, length us, event | category | flops | bytes accessed | tf_op | source)
XLA Modules:
  0.0 154.9 jit_solution(16348040853061811182)
XLA Ops:
  0.6 149.7 %backbone_and_heads.1 = (bf16[1728,128]{1,0:T(8,128)(2,1)S(1)}, bf16[1728,640]{1,0:T(8,128)(2,1)S(1)}, bf16[432,5120]{1,0:T(8,128)(2,1)S(1)}, bf16[432,5120]{1,0:T(8,128)(2,1)S(1)}) custom-call(bf16[1728,128]{1,0:T(8,128)(2,1)} %bitcast.5, bf16[1728,640]{1,0:T(8,128)(2,1)} %down_h.1, bf16[1024,640]{1,0:T(8,128)(2,1)} %resid.1, bf16[1024,640]{1,0:T(8,128)(2,1)} %grad.1, ...), custom_call_target="tpu_custom_call" | custom-call | tf_op jit(solution)/shard_map/backbone_and_heads/pallas_call | solution.py:584
  150.4 4.4 %place_results.1 = (bf16[1728,128]{1,0:T(8,128)(2,1)}, bf16[1728,640]{1,0:T(8,128)(2,1)}, bf16[432,5120]{1,0:T(8,128)(2,1)}, bf16[432,5120]{1,0:T(8,128)(2,1)}) custom-call(bf16[1728,128]{1,0:T(8,128)(2,1)S(1)} %get-tuple-element.12.refs_0_, bf16[1728,640]{1,0:T(8,128)(2,1)S(1)} %get-tuple-element.13.refs_1_, ...), custom_call_target="tpu_custom_call" | custom-call | tf_op jit(solution)/shard_map/place_results/pallas_call | solution.py:658

commit v5 on v4

--- a/solution.py
+++ b/solution.py
@@ -148,6 +148,9 @@
     vx = Copies(v_s, v_r)
 
     low, high = pl.ds(0, part), pl.ds(part, part)
+    by_x = inner // 6 // 16 * 16
+    low_x, low_y = pl.ds(0, by_x), pl.ds(by_x, part - by_x)
+    high_x, high_y = pl.ds(part, by_x), pl.ds(part + by_x, part - by_x)
 
     def pass_hidden(k, shard, rows_of, to):
         piece = hid.at[shard, rows_of]
@@ -244,11 +247,13 @@
         a.arrived(5)
         pass_hidden(7, after, high, ym)
         a.arrived(0)
-        pass_hidden(8, beside, low, yp)
+        pass_hidden(14, before, low_x, xp)
+        pass_hidden(15, after, high_x, xp)
+        pass_hidden(8, beside, low_y, yp)
         pass_hidden(10, beside, low, ym)
         a.arrived(1)
         pass_hidden(9, beside, high, yp)
-        pass_hidden(11, beside, high, ym)
+        pass_hidden(11, beside, high_y, ym)
         multiply(1)
         pass_on(0)
         a.arrived(3)
@@ -270,9 +275,9 @@
         cot_ring.share(BELOW)
         cot_ring.share(ABOVE)
     with jax.named_scope("gather_rest"):
-        a.arrived(8, 9)
+        a.arrived(8, 9, 14)
         multiply(5)
-        a.arrived(10, 11)
+        a.arrived(10, 11, 15)
         multiply(6)
         pass_on(5)
         pass_on(6)
@@ -574,7 +579,7 @@
     vmem = pl.BlockSpec(memory_space=pltpu.VMEM)
     dma = pltpu.SemaphoreType.DMA
     sems = []
-    for n in ((14,), (7,), (28,), (8,)):
+    for n in ((16,), (7,), (28,), (8,)):
         sems += [dma(n), dma(n)]
     sems += [dma((8,)), dma((2, 4))]
     for n in ((2,), (7,), (28,), (8,), (8,), (8,), (8,), (7,), (2,), (10,), (28,), (7,)):

time: 155 us -> 154 us (level)
  no operation moved by 1% of the time
where the time goes in v5:
time: 154 us
  Pallas kernels  153 us (99%)
    pallas_call x1, Pallas kernels, run(): pl.pallas_call(kernel, out_shape=(pltpu.VMEM((inner, tokens), BF16), pltp...  149 us
    pallas_call x1, Pallas kernels, place_results(): pl.pallas_call(copy_kernel, out_shape=tuple((jax.ShapeDtypeStruct(a.shape...  4.39 us

profile of v5, /device:TPU:1, one launch (start us, length us, event | category | flops | bytes accessed | tf_op | source)
XLA Modules:
  0.0 154.1 jit_solution(10631666648101699782)
XLA Ops:
  0.6 148.9 %backbone_and_heads.1 = (bf16[1728,128]{1,0:T(8,128)(2,1)S(1)}, bf16[1728,640]{1,0:T(8,128)(2,1)S(1)}, bf16[432,5120]{1,0:T(8,128)(2,1)S(1)}, bf16[432,5120]{1,0:T(8,128)(2,1)S(1)}) custom-call(bf16[1728,128]{1,0:T(8,128)(2,1)} %bitcast.5, bf16[1728,640]{1,0:T(8,128)(2,1)} %down_h.1, bf16[1024,640]{1,0:T(8,128)(2,1)} %resid.1, bf16[1024,640]{1,0:T(8,128)(2,1)} %grad.1, ...), custom_call_target="tpu_custom_call" | custom-call | tf_op jit(solution)/shard_map/backbone_and_heads/pallas_call | solution.py:589
  149.6 4.4 %place_results.1 = (bf16[1728,128]{1,0:T(8,128)(2,1)}, bf16[1728,640]{1,0:T(8,128)(2,1)}, bf16[432,5120]{1,0:T(8,128)(2,1)}, bf16[432,5120]{1,0:T(8,128)(2,1)}) custom-call(bf16[1728,128]{1,0:T(8,128)(2,1)S(1)} %get-tuple-element.12.refs_0_, bf16[1728,640]{1,0:T(8,128)(2,1)S(1)} %get-tuple-element.13.refs_1_, ...), custom_call_target="tpu_custom_call" | custom-call | tf_op jit(solution)/shard_map/place_results/pallas_call | solution.py:663
